TPU v7x, 256 devices: a whole 4x4x8 slice. The times are simulated.
256 devices in a mesh: seq: 32 (over z, x), exp: 8 (over y, core).
Axes of the slice: x: 4, y: 4, z: 8, core: 2. Of those that a mesh axis runs over, the one named last changes fastest.
Arguments:
- residual: bfloat16 [4096, 4096], P('seq', 'exp'), may hold values from -6 to 6
- query_proj: bfloat16 [4096, 4096], P('seq', 'exp'), may hold values from -6 to 6
- key_proj: bfloat16 [4096, 4096], P('seq', 'exp'), may hold values from -6 to 6
- value_proj: bfloat16 [4096, 4096], P('seq', 'exp'), may hold values from -6 to 6
- short_kernel: float32 [3, 3, 4096], P(None, None, 'exp'), may hold values from -3 to 3
- filter_raw: float32 [4096, 8, 512], P(None, 'exp', 'seq'), may hold values from -6 to 6
- filter_decay: float32 [8, 512], P('exp', 'seq'), may hold values from 4.8828124e-06 to 0.03
- routes: int32 [4096, 2], P('seq'), may hold values from 0 to 7, all different within a row; in each aligned block of 128 rows (0 to 127, 128 to 255, ...) at most 40 rows name the same one
- gate_weights: float32 [4096, 2], P('seq'), may hold values from 0.3 to 1
- norm_gain: float32 [4096], replicated, may hold values from 0.5 to 1.5
- w_gate: bfloat16 [8, 4096, 11008], P('exp', None, 'seq'), may hold values from -0.09375 to 0.09375
- w_up: bfloat16 [8, 4096, 11008], P('exp', None, 'seq'), may hold values from -0.09375 to 0.09375
- w_down: bfloat16 [8, 11008, 4096], P('exp', 'seq'), may hold values from -0.0546875 to 0.0546875
Outputs:
- block_out: bfloat16 [4096, 4096], P('seq', 'exp')
Inputs may be any that keep to these rules, and one draw needn't show every extreme that they name: `routes`: the 2 ids of a row differ. In each aligned block of 128 rows (the tokens of one index of seq) no expert is named by more than 40 rows, a bound that some block reaches.
All inputs are finite; a program needn't handle non-finite values.
Results may differ from a plain program's by a relative error of at most 0.015.
Values may be sent and summed in bfloat16 or wider, within the bound.
A program may use at most 128 MiB of HBM per device.

v0:
```python
import math

import jax
import jax.numpy as jnp
from jax import lax
from jax.sharding import PartitionSpec as P


def passed_along(value, axis, by):
    devices = lax.axis_size(axis)
    pairs = [(i, i + by) for i in range(devices) if 0 <= i + by < devices]
    return lax.ppermute(value, axis, pairs)


def short_filter(extended, kernel, length):
    tap_count = kernel.shape[0]
    signal = extended.astype(jnp.float32)
    running = kernel[0] * signal[tap_count - 1 : tap_count - 1 + length]
    for offset in range(1, tap_count):
        running = (
            running
            + kernel[offset] * signal[tap_count - 1 - offset : tap_count - 1 - offset + length]
        )
    return running


def with_zeros(signal, tap_count):
    return jnp.concatenate(
        (jnp.zeros((tap_count - 1, signal.shape[1]), signal.dtype), signal), axis=0
    )


def long_filter(raw_taps, decay_rate, length):
    positions = jnp.arange(length).astype(jnp.float32)[:, None]
    energy = jnp.expm1(-2.0 * decay_rate * length) / jnp.expm1(-2.0 * decay_rate)
    return raw_taps * jnp.exp(-decay_rate * positions) / jnp.sqrt(energy)


def rms_rows(rows_in, norm_gain):
    values = rows_in.astype(jnp.float32)
    square = jnp.mean(values * values, axis=-1, keepdims=True)
    return (values * lax.rsqrt(square + 1e-06) * norm_gain).astype(jnp.bfloat16)


def angle_table(row_total, col_total, period):
    product = (
        jnp.arange(row_total, dtype=jnp.int32)[:, None]
        * jnp.arange(col_total, dtype=jnp.int32)[None, :]
        % period
    )
    theta = product.astype(jnp.float32) * (2.0 * math.pi / period)
    return (jnp.cos(theta), jnp.sin(theta))


def left_real(tables, direction, real_part):
    cosine, sine = tables
    highest = lax.Precision.HIGHEST
    cos_real = jnp.einsum("kn,cnm->ckm", cosine, real_part, precision=highest)
    sin_real = jnp.einsum("kn,cnm->ckm", sine, real_part, precision=highest)
    return (cos_real, -direction * sin_real)


def left_real_out(tables, direction, real_part, imag_part):
    cosine, sine = tables
    highest = lax.Precision.HIGHEST
    cos_real = jnp.einsum("kn,cnm->ckm", cosine, real_part, precision=highest)
    sin_imag = jnp.einsum("kn,cnm->ckm", sine, imag_part, precision=highest)
    return cos_real + direction * sin_imag


def right_apply(tables, direction, real_part, imag_part):
    cosine, sine = tables
    highest = lax.Precision.HIGHEST
    cos_real = jnp.einsum("ckn,nm->ckm", real_part, cosine, precision=highest)
    cos_imag = jnp.einsum("ckn,nm->ckm", imag_part, cosine, precision=highest)
    sin_real = jnp.einsum("ckn,nm->ckm", real_part, sine, precision=highest)
    sin_imag = jnp.einsum("ckn,nm->ckm", imag_part, sine, precision=highest)
    return (cos_real + direction * sin_imag, cos_imag - direction * sin_real)


def twist(tables, direction, real_part, imag_part):
    cosine, sine = tables
    return (
        real_part * cosine + direction * imag_part * sine,
        imag_part * cosine - direction * real_part * sine,
    )


def causal_conv(signal, taps):
    channel_count, length = signal.shape
    padded_size = 2 * length
    second = 128
    first = padded_size // second
    first_tab = angle_table(first, first, first)
    second_tab = angle_table(second, second, second)
    twist_tab = angle_table(first, second, padded_size)
    both = jnp.concatenate((signal, taps), axis=0)
    real_part = jnp.pad(both, ((0, 0), (0, length))).reshape(2 * channel_count, first, second)
    real_part, imag_part = left_real(first_tab, 1.0, real_part)
    real_part, imag_part = twist(twist_tab, 1.0, real_part, imag_part)
    real_part, imag_part = right_apply(second_tab, 1.0, real_part, imag_part)
    sig_real, tap_real = (real_part[:channel_count], real_part[channel_count:])
    sig_imag, tap_imag = (imag_part[:channel_count], imag_part[channel_count:])
    prod_real = sig_real * tap_real - sig_imag * tap_imag
    prod_imag = sig_real * tap_imag + sig_imag * tap_real
    real_part, imag_part = right_apply(second_tab, -1.0, prod_real, prod_imag)
    real_part, imag_part = twist(twist_tab, -1.0, real_part, imag_part)
    real_part = left_real_out(first_tab, -1.0, real_part, imag_part)
    return real_part.reshape(channel_count, padded_size)[:, :length] / padded_size


def on_device(
    residual,
    query_proj,
    key_proj,
    value_proj,
    short_kernel,
    filter_raw,
    filter_decay,
    routes,
    gate_weights,
    norm_gain,
    w_gate,
    w_up,
    w_down,
):
    row_count, width_here = query_proj.shape
    tap_count = short_kernel.shape[1]
    seq_total = lax.axis_size("seq")
    exp_total = lax.axis_size("exp")
    length = row_count * seq_total
    slice_width = width_here // seq_total
    stacked = query_proj[None]
    rims = passed_along(stacked[:, row_count - (tap_count - 1) :], "seq", 1)
    extended = jnp.concatenate((rims, stacked), axis=1)
    query_short = short_filter(extended[0], short_kernel[0], row_count)
    key_full, value_full = (
        lax.all_to_all(key_proj, "seq", split_axis=1, concat_axis=0, tiled=True),
        lax.all_to_all(value_proj, "seq", split_axis=1, concat_axis=0, tiled=True),
    )
    kernel_here = lax.dynamic_slice_in_dim(
        short_kernel, lax.axis_index("seq") * slice_width, slice_width, 2
    )
    key_short = short_filter(with_zeros(key_full, tap_count), kernel_here[1], length)
    value_short = short_filter(with_zeros(value_full, tap_count), kernel_here[2], length)
    zed = (key_short * value_short).astype(jnp.bfloat16)
    taps = long_filter(
        filter_raw.reshape(length, slice_width), filter_decay.reshape(slice_width), length
    )
    conv_cols = causal_conv(zed.astype(jnp.float32).T, taps.T)
    conv_here = conv_cols.T.astype(jnp.bfloat16)
    conv = lax.all_to_all(conv_here, "seq", split_axis=0, concat_axis=1, tiled=True)
    mixed = (residual.astype(jnp.float32) + query_short * conv.astype(jnp.float32)).astype(
        jnp.bfloat16
    )
    local_experts = w_gate.shape[0]
    expert_count = local_experts * exp_total
    topk_count = routes.shape[1]
    capacity = 5 * row_count * topk_count // (4 * expert_count)
    expert_hot = (routes[:, :, None] == jnp.arange(expert_count, dtype=jnp.int32)).astype(jnp.int32)
    per_token = jnp.sum(expert_hot, axis=1)
    earlier = jnp.cumsum(per_token, axis=0) - per_token
    slot_index = jnp.sum(expert_hot * earlier[:, None, :], axis=2)
    slot_hot = (slot_index[:, :, None] == jnp.arange(capacity, dtype=jnp.int32)).astype(jnp.float32)
    hot_float = expert_hot.astype(jnp.float32)
    placement_map = jnp.einsum("tke,tkc->ect", hot_float, slot_hot)
    weight_map = jnp.einsum(
        "tke,tkc,tk->ect", hot_float, slot_hot, gate_weights, precision=lax.Precision.HIGHEST
    )
    outgoing = jnp.einsum(
        "ect,td->ecd", placement_map.astype(jnp.bfloat16), mixed, preferred_element_type=jnp.float32
    ).astype(jnp.bfloat16)
    arrived = lax.all_to_all(outgoing, "exp", split_axis=0, concat_axis=2, tiled=True)
    normed = rms_rows(lax.all_gather(arrived, "seq", axis=1, tiled=True), norm_gain)
    gate_act = jnp.einsum("end,edf->nef", normed, w_gate, preferred_element_type=jnp.float32)
    up_act = jnp.einsum("end,edf->nef", normed, w_up, preferred_element_type=jnp.float32)
    hidden = (jax.nn.silu(gate_act) * up_act).astype(jnp.bfloat16)
    summed = lax.psum_scatter(
        jnp.einsum("nef,efd->ned", hidden, w_down, preferred_element_type=jnp.float32).astype(
            jnp.bfloat16
        ),
        "seq",
        scatter_dimension=0,
        tiled=True,
    )
    returned = lax.all_to_all(summed, "exp", split_axis=2, concat_axis=1, tiled=True)
    combined = jnp.einsum(
        "ect,ced->td", weight_map, returned.astype(jnp.float32), precision=lax.Precision.HIGHEST
    )
    return (mixed.astype(jnp.float32) + combined).astype(jnp.bfloat16)


def solution(mesh):
    in_specs = (
        P("seq", "exp"),
        P("seq", "exp"),
        P("seq", "exp"),
        P("seq", "exp"),
        P(None, None, "exp"),
        P(None, "exp", "seq"),
        P("exp", "seq"),
        P("seq", None),
        P("seq", None),
        P(),
        P("exp", None, "seq"),
        P("exp", None, "seq"),
        P("exp", "seq", None),
    )
    out_specs = P("seq", "exp")
    return jax.shard_map(
        on_device, mesh=mesh, in_specs=in_specs, out_specs=out_specs, check_vma=False
    )
```

profile of v0, /device:TPU:1, one launch (start us, length us, event | category | flops | bytes accessed | tf_op | source)
XLA Modules:
  0.0 535.0 jit_solution(7284293284483902443)
XLA Ops:
  6.5 1.8 copy.41
  8.4 11.9 %all-to-all-start.1 = ((bf16[128,32,16]{0,2,1:T(8,128)(2,1)}), bf16[128,32,16]{0,2,1:T(8,128)(2,1)S(1)}, u32[]{:S(2)}, u32[]{:S(2)}) async-start(bf16[128,32,16]{0,2,1:T(8,128)(2,1)} %bitcast.13), calls=%async_computation.1 | async-start | bytes 262144 | tf_op jit(solution)/shard_map/all_to_all | solution.py:139
  20.2 1.3 slice.129
  21.5 3.7 collective-permute-start
  25.5 1.2 negate_bitcast_fusion
  26.7 0.8 copy.45
  28.0 2.4 select_reduce_fusion
  30.4 1.1 fusion.73
  31.5 1.5 dynamic-slice_bitcast_fusion.5
  33.0 1.7 copy.39
  34.6 1.5 fusion.43
  36.2 8.6 %all-to-all-start = ((bf16[128,32,16]{0,2,1:T(8,128)(2,1)}), bf16[128,32,16]{0,2,1:T(8,128)(2,1)}, u32[]{:S(2)}, u32[]{:S(2)}) async-start(bf16[128,32,16]{0,2,1:T(8,128)(2,1)} %bitcast.8), calls=%async_computation | async-start | bytes 262144 | tf_op jit(solution)/shard_map/all_to_all | solution.py:138
  44.8 9.1 %all-to-all-done = bf16[128,32,16]{0,2,1:T(8,128)(2,1)} async-done(((bf16[128,32,16]{0,2,1:T(8,128)(2,1)}), bf16[128,32,16]{0,2,1:T(8,128)(2,1)}, u32[]{:S(2)}, u32[]{:S(2)}) %all-to-all-start) | async-done | bytes 131104 | tf_op jit(solution)/shard_map/all_to_all | solution.py:138
  54.0 0.9 copy_bitcast_fusion.2
  55.0 1.0 convert_bitcast_fusion
  56.3 1.2 convolution_bitcast_fusion
  57.5 1.2 convolution_bitcast_fusion.1
  58.7 1.2 fusion.55
  59.9 1.2 fusion.56
  61.1 1.2 convolution_add_fusion
  62.4 1.2 convolution_subtract_fusion
  63.9 0.8 fusion.91
  64.7 0.8 fusion.89
  65.5 0.8 fusion.42
  66.3 0.8 fusion.41
  67.2 1.0 fusion.51
  70.0 3.9 all-to-all-start.2
  73.9 0.8 fusion.188
  75.4 7.8 %all-to-all-done.2 = bf16[32,128,16]{1,2,0:T(8,128)(2,1)S(1)} async-done(((bf16[32,128,16]{1,2,0:T(8,128)(2,1)}), bf16[32,128,16]{1,2,0:T(8,128)(2,1)S(1)}, u32[]{:S(2)}, u32[]{:S(2)}) %all-to-all-start.2) | async-done | bytes 131104 | tf_op jit(solution)/shard_map/all_to_all | solution.py:152
  84.0 1.1 copy.44
  85.1 1.0 fusion.68
  86.1 1.2 convolution_convert_fusion.1
  87.3 16.0 %all_to_all.81 = bf16[8,40,512]{2,1,0:T(8,128)(2,1)S(1)} all-to-all(bf16[8,40,512]{2,1,0:T(8,128)(2,1)S(1)} %convolution_convert_fusion.1), channel_id=1, replica_groups=mesh['seq'=32,'exp'=8] {'exp'}, dimensions={0} | all-to-all | bytes 655360 | tf_op jit(solution)/shard_map/all_to_all | solution.py:173
  104.1 101.8 %all-gather.2.cloned.1.call-done = bf16[1,1280,4096]{2,1,0:T(8,128)(2,1)} async-done(((bf16[1,40,4096]{2,1,0:T(8,128)(2,1)}), bf16[1,1280,4096]{2,1,0:T(8,128)(2,1)}) %all-gather.2.cloned.1.call-update) | async-done | bytes 10485776 | tf_op jit(solution)/shard_map/all_gather | solution.py:174
  206.0 6.2 %fusion = f32[1280]{0:T(1024)S(1)} fusion(bf16[1,1280,4096]{2,1,0:T(8,128)(2,1)} %all-gather.2.cloned.1.call-done), kind=kLoop, calls=%fused_computation.2 | loop fusion | flops 15727360 | bytes 10490880 | tf_op jit(solution)/shard_map/reduce_sum | solution.py:41
  212.9 7.0 %fusion.9 = f32[1280,1,344]{0,2,1:T(8,128)} fusion(bf16[1,1280,4096]{2,1,0:T(8,128)(2,1)S(1)} %copy-done.1, f32[4096]{0:T(1024)S(1)} %copy-done.8, f32[1280]{0:T(1024)S(1)} %add_rsqrt_fusion, bf16[1,4096,344]{1,2,0:T(8,128)(2,1)} %param.23), kind=kOutput, calls=%fused_computation.10 | convolution fusion | flops 3628072960 | bytes 15086592 | tf_op jit(solution)/shard_map/end,edf->nef/dot_general | solution.py:175
  219.9 20.0 %fusion.3 = bf16[1280,1,4096]{2,0,1:T(8,128)(2,1)} fusion(bf16[1,344,4096]{2,1,0:T(8,128)(2,1)S(1)} %copy-done, bf16[1,4096,344]{1,2,0:T(8,128)(2,1)} %param.24, bf16[1,1280,4096]{2,1,0:T(8,128)(2,1)} %all-gather.2.cloned.1.call-done, f32[4096]{0:T(1024)S(1)} %copy-done.8, f32[1280]{0:T(1024)S(1)} %add_rsqrt_fusion, f32[1280,1,344]{0,2,1:T(8,128)} %fusion.9), kind=kOutput, calls=%fused_computation.6 | convolution fusion | flops 7243059200 | bytes 28390400 | tf_op jit(solution)/shard_map/nef,efd->ned/dot_general | solution.py:179
  239.9 227.7 %reduce-scatter.2.cloned.1.call-done = bf16[40,1,4096]{2,0,1:T(8,128)(2,1)} async-done(((bf16[1280,1,4096]{2,0,1:T(8,128)(2,1)}), bf16[40,1,4096]{2,0,1:T(8,128)(2,1)}) %reduce-scatter.2.cloned.1.call-update) | async-done | bytes 327696 | tf_op jit(solution)/shard_map/reduce_scatter | solution.py:178
  467.6 5.1 copy.49
  473.2 24.4 %reduce.1 = bf16[4096,40]{1,0:T(8,128)(2,1)} reduce(bf16[4096,1,40]{2,1,0:T(2,128)(2,1)} %bitcast.215, bf16[]{:T(256)} %broadcast.201), dimensions={1}, to_apply=%bitcast.196.reduce_sub_computation | reduce | bytes 655362
  497.6 3.8 reshape.148
  501.5 9.0 %all-to-all-start.4 = ((bf16[8,2,10240]{2,1,0:T(2,128)(2,1)}), bf16[8,2,10240]{2,1,0:T(2,128)(2,1)S(1)}, u32[]{:S(2)}, u32[]{:S(2)}) async-start(bf16[8,2,10240]{2,1,0:T(2,128)(2,1)} %reshape.148), calls=%async_computation.5 | async-start | bytes 655360 | tf_op jit(solution)/shard_map/all_to_all | solution.py:186
  510.6 2.3 convolution_bitcast_fusion.2
  512.9 1.2 copy.51
  514.1 3.4 all-to-all-done.4
  517.6 4.7 reshape.149
  522.3 4.5 copy.50
  526.9 1.1 fusion.45
  (45 shorter events, 6.9 us)
Async XLA Ops:
  6.5 213.4 %copy-start = (bf16[1,344,4096]{2,1,0:T(8,128)(2,1)S(1)}, bf16[1,344,4096]{2,1,0:T(8,128)(2,1)}, u32[]{:S(2)}) copy-start(bf16[1,344,4096]{2,1,0:T(8,128)(2,1)} %param.25) | copy-start | bytes 8454148
  8.4 27.8 %all-to-all-start.1 = ((bf16[128,32,16]{0,2,1:T(8,128)(2,1)}), bf16[128,32,16]{0,2,1:T(8,128)(2,1)S(1)}, u32[]{:S(2)}, u32[]{:S(2)}) async-start(bf16[128,32,16]{0,2,1:T(8,128)(2,1)} %bitcast.13), calls=%async_computation.1 | async-start | bytes 262144 | tf_op jit(solution)/shard_map/all_to_all | solution.py:139
  21.5 53.2 %collective-permute-start = (bf16[1,2,512]{2,1,0:T(2,128)(2,1)}, bf16[1,2,512]{2,1,0:T(2,128)(2,1)}, u32[]{:S(2)}, u32[]{:S(2)}) collective-permute-start(bf16[1,2,512]{2,1,0:T(2,128)(2,1)} %slice.129), channel_id=1, source_target_pairs={{0,8},{8,16},{16,24},{24,32},{32,40},{40,48},{48,56},{56,64},{64,7... | collective-permute-start | bytes 6152 | tf_op jit(solution)/shard_map/ppermute | solution.py:12
  27.5 28.5 %copy-start.2 = (s32[128,2]{1,0:T(8,128)}, s32[128,2]{1,0:T(8,128)S(1)}, u32[]{:S(2)}) copy-start(s32[128,2]{1,0:T(8,128)S(1)} %copy.45) | copy-start | bytes 3076
  30.4 5.8 %copy-start.5 = (s32[128,2]{1,0:T(8,128)}, s32[128,2]{1,0:T(8,128)S(1)}, u32[]{:S(2)}) copy-start(s32[128,2]{1,0:T(8,128)S(1)} %select_reduce_fusion) | copy-start | bytes 3076
  36.2 17.8 %all-to-all-start = ((bf16[128,32,16]{0,2,1:T(8,128)(2,1)}), bf16[128,32,16]{0,2,1:T(8,128)(2,1)}, u32[]{:S(2)}, u32[]{:S(2)}) async-start(bf16[128,32,16]{0,2,1:T(8,128)(2,1)} %bitcast.8), calls=%async_computation | async-start | bytes 262144 | tf_op jit(solution)/shard_map/all_to_all | solution.py:138
  67.2 7.6 %copy-start.4 = (bf16[128,512]{1,0:T(8,128)(2,1)S(1)}, bf16[128,512]{1,0:T(8,128)(2,1)}, u32[]{:S(2)}) copy-start(bf16[128,512]{1,0:T(8,128)(2,1)} %param.14) | copy-start | bytes 393220
  70.0 13.3 %all-to-all-start.2 = ((bf16[32,128,16]{1,2,0:T(8,128)(2,1)}), bf16[32,128,16]{1,2,0:T(8,128)(2,1)S(1)}, u32[]{:S(2)}, u32[]{:S(2)}) async-start(bf16[32,128,16]{1,2,0:T(8,128)(2,1)} %copy_bitcast_fusion.3), calls=%async_computation.2 | async-start | bytes 262144 | tf_op jit(solution)/shard_map/all_to_all | solution.py:152
  73.9 132.1 %all-gather.2.cloned.1.call-start = ((), (), s32[]{:S(2)}) async-start(), calls=%async_computation.6 | async-start | bytes 10813440 | tf_op jit(solution)/shard_map/all_gather | solution.py:174
  104.1 108.1 %copy-start.8 = (f32[4096]{0:T(1024)S(1)}, f32[4096]{0:T(1024)}, u32[]{:S(2)}) copy-start(f32[4096]{0:T(1024)} %param.22) | copy-start | bytes 49156
  104.1 363.5 %reduce-scatter.2.cloned.1.call-start = ((), (), s32[]{:S(2)}) async-start(), calls=%async_computation.7 | async-start | bytes 10813440 | tf_op jit(solution)/shard_map/reduce_scatter | solution.py:178
  206.0 7.0 %copy-start.1 = (bf16[1,1280,4096]{2,1,0:T(8,128)(2,1)S(1)}, bf16[1,1280,4096]{2,1,0:T(8,128)(2,1)}, u32[]{:S(2)}) copy-start(bf16[1,1280,4096]{2,1,0:T(8,128)(2,1)} %all-gather.2.cloned.1.call-done) | copy-start | bytes 31457284
  472.7 37.8 %copy-start.7 = (f32[128,2]{0,1:T(2,128)S(1)}, f32[128,2]{0,1:T(2,128)}, u32[]{:S(2)}) copy-start(f32[128,2]{0,1:T(2,128)} %param.21) | copy-start | bytes 3076
  472.7 37.9 %copy-start.3 = (s32[128,2]{1,0:T(8,128)S(1)}, s32[128,2]{1,0:T(8,128)}, u32[]{:S(2)}) copy-start(s32[128,2]{1,0:T(8,128)} %copy-done.2) | copy-start | bytes 3076
  472.7 37.9 %copy-start.6 = (s32[128,2]{1,0:T(8,128)S(1)}, s32[128,2]{1,0:T(8,128)}, u32[]{:S(2)}) copy-start(s32[128,2]{1,0:T(8,128)} %copy-done.5) | copy-start | bytes 3076
  501.5 16.1 %all-to-all-start.4 = ((bf16[8,2,10240]{2,1,0:T(2,128)(2,1)}), bf16[8,2,10240]{2,1,0:T(2,128)(2,1)S(1)}, u32[]{:S(2)}, u32[]{:S(2)}) async-start(bf16[8,2,10240]{2,1,0:T(2,128)(2,1)} %reshape.148), calls=%async_computation.5 | async-start | bytes 655360 | tf_op jit(solution)/shard_map/all_to_all | solution.py:186
Sparse Core Ops, SparseCore 0:
  104.2 101.7 all-gather.1
  240.1 227.4 reduce-scatter.1
where the time goes:
time: 541 us; the launch traced here: 535 us
  waiting for transfers between devices  350 us (65%)
  matrix products  45.5 us (8%)
  other arithmetic  40.7 us (8%)
  starting transfers between devices  37.1 us (7%)
  local copies, waits for them, and re-layouts  31.9 us (6%)
  blocking collectives  16 us (3%)
  between operations  13.9 us (3%)
    reduce_scatter x1, waiting for transfers between devices, on_device(): lax.psum_scatter(jnp.einsum('nef,efd->ned', hidden, w_down, preferred_ele...  228 us
    all_gather x1, waiting for transfers between devices, on_device(): lax.all_gather(arrived, 'seq', axis=1, tiled=True)  102 us
    unnamed x2, other arithmetic  24.5 us
    dot_general x1, matrix products, on_device(): jnp.einsum('nef,efd->ned', hidden, w_down, preferred_element_type=jnp.flo...  20 us
    all_to_all x1, blocking collectives, on_device(): lax.all_to_all(outgoing, 'exp', split_axis=0, concat_axis=2, tiled=True)  16 us
    unnamed x28, local copies, waits for them, and re-layouts  14.8 us
    all_to_all x1, starting transfers between devices, on_device(): lax.all_to_all(value_proj, 'seq', split_axis=1, concat_axis=0, tiled=True)  11.9 us
  transfers between devices with their start and end apart: 7, of which 5 were waited for; matrix products, arithmetic and copies ran while one was open for 6% of the time, Pallas kernels for 0%

commit v1 on v0

--- a/solution.py
+++ b/solution.py
@@ -1,9 +1,15 @@
+import functools
 import math
 
 import jax
 import jax.numpy as jnp
 from jax import lax
+from jax.experimental import pallas as pl
+from jax.experimental.pallas import tpu as pltpu
 from jax.sharding import PartitionSpec as P
+
+MESH = pl.DeviceIdType.MESH
+F32, BF16 = jnp.float32, jnp.bfloat16
 
 
 def passed_along(value, axis, by):
@@ -34,12 +40,6 @@
     positions = jnp.arange(length).astype(jnp.float32)[:, None]
     energy = jnp.expm1(-2.0 * decay_rate * length) / jnp.expm1(-2.0 * decay_rate)
     return raw_taps * jnp.exp(-decay_rate * positions) / jnp.sqrt(energy)
-
-
-def rms_rows(rows_in, norm_gain):
-    values = rows_in.astype(jnp.float32)
-    square = jnp.mean(values * values, axis=-1, keepdims=True)
-    return (values * lax.rsqrt(square + 1e-06) * norm_gain).astype(jnp.bfloat16)
 
 
 def angle_table(row_total, col_total, period):
@@ -107,6 +107,352 @@
     real_part, imag_part = twist(twist_tab, -1.0, real_part, imag_part)
     real_part = left_real_out(first_tab, -1.0, real_part, imag_part)
     return real_part.reshape(channel_count, padded_size)[:, :length] / padded_size
+
+
+def expert_kernel(
+    dims,
+    mixed_ref, place_ref, wmap_ref, gain_ref, wg_hbm, wu_hbm, wd_hbm, out_ref,
+    wg, wu, wd, outg, arr, xa, xb, acc_g, acc_u, hid, pc, pd, rc1, rc2, rd1, rd2, yb, ret,
+    w_sem, go_send, go_recv, a_recv, b_recv, rc1_recv, rc2_recv, rd1_recv, rd2_recv, back_send, back_recv,
+    az_send, ax_send, bz_send, bx_send, cz_send, cx_send, dz_send, dx_send,
+):
+    nz, nx, ne, cap, wa, wb = dims
+    width = 2 * (wa + wb)
+    chunk = width // ne
+    s, e = lax.axis_index("seq"), lax.axis_index("exp")
+    z, x = s // nx, s % nx
+
+    def along_z(d):
+        return (((z + (1, nz - 1)[d]) % nz) * nx + x, e)
+
+    def along_x(d):
+        return (z * nx + (x + (1, nx - 1)[d]) % nx, e)
+
+    def expert(i):
+        return (s, (e + i) % ne)
+
+    def remote(src, dst, send, recv, to):
+        return pltpu.make_async_remote_copy(
+            src_ref=src, dst_ref=dst, send_sem=send, recv_sem=recv, device_id=to, device_id_type=MESH
+        )
+
+    def arrived(dst, recv):
+        remote(dst, dst, recv, recv, along_z(0)).wait_recv()
+
+    def sent(src, send):
+        remote(src, src, send, send, along_z(0)).wait_send()
+
+    weights = [
+        pltpu.make_async_copy(h.at[0], v, w_sem.at[i]) for i, (h, v) in enumerate(((wg_hbm, wg), (wu_hbm, wu), (wd_hbm, wd)))
+    ]
+    for copy in weights:
+        copy.start()
+
+    barrier = pltpu.get_barrier_semaphore()
+    partners = [along_z(0), along_z(1), along_x(0), along_x(1)] + [expert(i) for i in range(1, ne)]
+    for to in partners:
+        pl.semaphore_signal(barrier, inc=1, device_id=to, device_id_type=MESH)
+    picked = jnp.dot(place_ref[...], mixed_ref[...], preferred_element_type=F32)
+    outg[...] = picked.reshape(ne, cap, chunk).astype(BF16)
+    arr[e] = outg[e]
+    acc_g[...] = jnp.zeros_like(acc_g)
+    acc_u[...] = jnp.zeros_like(acc_u)
+    pl.semaphore_wait(barrier, len(partners))
+
+    for i in range(1, ne):
+        remote(outg.at[(e + i) % ne], arr.at[e], go_send.at[i], go_recv.at[i], expert(i)).start()
+    for i in range(1, ne):
+        arrived(arr.at[(e + ne - i) % ne], go_recv.at[i])
+    square = jnp.zeros((cap, 1), F32)
+    for c in range(ne):
+        values = arr[c].astype(F32)
+        square += jnp.sum(values * values, axis=-1, keepdims=True)
+    scale = lax.rsqrt(square / width + 1e-06)
+    spans = []
+    for d in range(2):
+        spans.append((xa, pc, d, d * wa, wa))
+        spans.append((xb, pd, d, 2 * wa + d * wb, wb))
+    for c in range(ne):
+        values = (arr[c].astype(F32) * scale * gain_ref[:, c * chunk : (c + 1) * chunk]).astype(BF16)
+        for ref, _, d, start, size in spans:
+            lo, hi = max(start, c * chunk), min(start + size, (c + 1) * chunk)
+            if lo < hi:
+                ref[d, 0, 0, :, lo - start : hi - start] = values[:, lo - c * chunk : hi - c * chunk]
+
+    def a_along_z(d, t, j):
+        remote(xa.at[d, t, j], xa.at[d, t + 1, j], az_send.at[d], a_recv.at[d, t + 1, j], along_z(d)).start()
+
+    def a_along_x(d, j):
+        remote(xa.at[d, 0, j], xa.at[d, 0, j + 1], ax_send.at[d], a_recv.at[d, 0, j + 1], along_x(d)).start()
+
+    def b_along_z(d, t):
+        remote(xb.at[d, t, 0], xb.at[d, t + 1, 0], bz_send.at[d], b_recv.at[d, t + 1, 0], along_z(d)).start()
+
+    def b_along_x(d, t, j):
+        remote(xb.at[d, t, j], xb.at[d, t, j + 1], bx_send.at[d], b_recv.at[d, t, j + 1], along_x(d)).start()
+
+    for d in range(2):
+        b_along_z(d, 0)
+        a_along_x(d, 0)
+    for d in range(2):
+        b_along_x(d, 0, 0)
+        a_along_z(d, 0, 0)
+
+    def turned(j, d):
+        return (nx - j) % nx if d else j
+
+    def rows_of(ref, d, t):
+        parts = [ref[d, t, turned(j, d)].astype(F32) for j in range(nx)]
+        return jnp.concatenate(parts, axis=0).astype(BF16)
+
+    def group(d, t):
+        return (nz - t) % nz if d else t
+
+    def project(d, t):
+        at = group(d, t)
+        left, right = rows_of(xa, d, t), rows_of(xb, d, t)
+        one = slice(d * wa, (d + 1) * wa)
+        two = slice(2 * wa + d * wb, 2 * wa + (d + 1) * wb)
+        for total, w in ((acc_g, wg), (acc_u, wu)):
+            total[at] += jnp.dot(left, w[one, :], preferred_element_type=F32) + jnp.dot(
+                right, w[two, :], preferred_element_type=F32
+            )
+
+    def activate(d, t):
+        at = group(d, t)
+        gate = acc_g[at]
+        hid[at] = (gate / (1.0 + jnp.exp(-gate)) * acc_u[at]).astype(BF16)
+
+    def gather_step(p, carry):
+        for d in range(2):
+            @pl.when(p <= nz - 1)
+            def _():
+                arrived(xb.at[d, p, 0], b_recv.at[d, p, 0])
+                b_along_x(d, p, 0)
+
+            @pl.when(p < nz - 1)
+            def _():
+                b_along_z(d, p)
+
+            @pl.when(p <= nx - 1)
+            def _():
+                arrived(xa.at[d, 0, p], a_recv.at[d, 0, p])
+                a_along_z(d, 0, p)
+
+            @pl.when(p < nx - 1)
+            def _():
+                a_along_x(d, p)
+
+        for j in range(nx):
+            for d in range(2):
+                t = p - j
+
+                @pl.when((t >= 1) & (t <= nz - 1))
+                def _():
+                    arrived(xa.at[d, t, j], a_recv.at[d, t, j])
+
+                @pl.when((t >= 1) & (t < nz - 1))
+                def _():
+                    a_along_z(d, t, j)
+
+            if j >= 1:
+                for d in range(2):
+                    t = p - j
+
+                    @pl.when((t >= 0) & (t <= nz - 1))
+                    def _():
+                        arrived(xb.at[d, t, j], b_recv.at[d, t, j])
+                        if j < nx - 1:
+                            b_along_x(d, t, j)
+
+        @pl.when(p == nx - 1)
+        def _():
+            for copy in weights:
+                copy.wait()
+
+        for d in range(2):
+            t = p - (nx - 1)
+
+            @pl.when(t >= 0)
+            def _():
+                project(d, t)
+
+            @pl.when((t > nz // 2) | ((t == 0) | (t == nz // 2)) & (d == 1))
+            def _():
+                activate(d, t)
+
+        return carry
+
+    lax.fori_loop(1, nz + nx - 1, gather_step, 0)
+
+    def down(d, q):
+        at = group(d, q % nz)
+        rows = hid[at]
+        for ref, start, size in ((pc, d * wa, wa), (pd, 2 * wa + d * wb, wb)):
+            part = jnp.dot(rows, wd[:, start : start + size], preferred_element_type=F32)
+            for j in range(nx):
+                ref[d, q - 1, turned(j, d)] = part[j * cap : (j + 1) * cap].astype(BF16)
+
+    def add(total, more):
+        total[...] = (total[...].astype(F32) + more[...].astype(F32)).astype(BF16)
+
+    for d in range(2):
+        down(d, 1)
+
+    def reduce_step(p, carry):
+        for d in range(2):
+            for v in range(1, nx + 1):
+                k, j = p - v + 1, v % nx
+
+                @pl.when((k >= 1) & (k <= nz))
+                def _():
+                    if v >= 2:
+                        arrived(rd1.at[d, v - 2, k - 1], rd1_recv.at[d, v - 2, k - 1])
+                        add(pd.at[d, k - 1, j], rd1.at[d, v - 2, k - 1])
+                    if v < nx:
+                        remote(
+                            pd.at[d, k - 1, j], rd1.at[d, v - 1, k - 1], dx_send.at[d], rd1_recv.at[d, v - 1, k - 1], along_x(d)
+                        ).start()
+                    else:
+                        @pl.when(k >= 2)
+                        def _():
+                            arrived(rd2.at[d, k - 2], rd2_recv.at[d, k - 2])
+                            add(pd.at[d, k - 1, 0], rd2.at[d, k - 2])
+
+                        @pl.when(k < nz)
+                        def _():
+                            remote(
+                                pd.at[d, k - 1, 0], rd2.at[d, k - 1], dz_send.at[d], rd2_recv.at[d, k - 1], along_z(d)
+                            ).start()
+
+        for d in range(2):
+            for v in range(1, nx + 1):
+                q, j = p - v + 1, v % nx
+
+                @pl.when((q >= 2) & (q <= nz))
+                def _():
+                    arrived(rc1.at[d, q - 2, j], rc1_recv.at[d, q - 2, j])
+                    add(pc.at[d, q - 1, j], rc1.at[d, q - 2, j])
+
+                @pl.when((q >= 1) & (q < nz))
+                def _():
+                    remote(
+                        pc.at[d, q - 1, j], rc1.at[d, q - 1, j], cz_send.at[d], rc1_recv.at[d, q - 1, j], along_z(d)
+                    ).start()
+
+                @pl.when(q == nz)
+                def _():
+                    if v >= 2:
+                        arrived(rc2.at[d, v - 2], rc2_recv.at[d, v - 2])
+                        add(pc.at[d, nz - 1, j], rc2.at[d, v - 2])
+                    if v < nx:
+                        remote(
+                            pc.at[d, nz - 1, j], rc2.at[d, v - 1], cx_send.at[d], rc2_recv.at[d, v - 1], along_x(d)
+                        ).start()
+
+        for d in range(2):
+            @pl.when(p < nz)
+            def _():
+                down(d, p + 1)
+
+        return carry
+
+    lax.fori_loop(1, nz + nx, reduce_step, 0)
+
+    for c in range(ne):
+        for _, ref, d, start, size in spans:
+            lo, hi = max(start, c * chunk), min(start + size, (c + 1) * chunk)
+            if lo < hi:
+                yb[c, :, lo - c * chunk : hi - c * chunk] = ref[d, nz - 1, 0, :, lo - start : hi - start]
+    for i in range(1, ne):
+        remote(yb.at[(e + i) % ne], ret.at[e], back_send.at[i], back_recv.at[i], expert(i)).start()
+    ret[e] = yb[e]
+    for d in range(2):
+        sent(xa.at[d, 0 : nz - 1], az_send.at[d])
+        sent(xa.at[d, 0, 0 : nx - 1], ax_send.at[d])
+        sent(xb.at[d, 0 : nz - 1, 0], bz_send.at[d])
+        sent(xb.at[d, :, 0 : nx - 1], bx_send.at[d])
+        sent(pc.at[d, 0 : nz - 1], cz_send.at[d])
+        sent(pc.at[d, nz - 1, 0 : nx - 1], cx_send.at[d])
+        sent(pd.at[d, 0 : nz - 1, 0], dz_send.at[d])
+        sent(pd.at[d, :, 0 : nx - 1], dx_send.at[d])
+    for i in range(1, ne):
+        sent(outg.at[i], go_send.at[i])
+    for i in range(1, ne):
+        arrived(ret.at[(e + ne - i) % ne], back_recv.at[i])
+    rows = ret[...].astype(F32).reshape(ne * cap, chunk)
+    combined = jnp.dot(wmap_ref[...], rows, preferred_element_type=F32, precision=lax.Precision.HIGHEST)
+    out_ref[...] = (mixed_ref[...].astype(F32) + combined).astype(BF16)
+    for i in range(1, ne):
+        sent(yb.at[i], back_send.at[i])
+
+
+def experts(mixed, place, wmap, gain, w_gate, w_up, w_down, nz, nx, parts):
+    ne = lax.axis_size("exp")
+    cap = place.shape[0] // ne
+    chunk = mixed.shape[1]
+    width = ne * chunk
+    wa, wb = parts
+    hidden = w_gate.shape[2]
+    vmem, dma = pltpu.VMEM, pltpu.SemaphoreType.DMA
+    scratch = [
+        vmem((width, hidden), BF16),
+        vmem((width, hidden), BF16),
+        vmem((hidden, width), BF16),
+        vmem((ne, cap, chunk), BF16),
+        vmem((ne, cap, chunk), BF16),
+        vmem((2, nz, nx, cap, wa), BF16),
+        vmem((2, nz, nx, cap, wb), BF16),
+        vmem((nz, nx * cap, hidden), F32),
+        vmem((nz, nx * cap, hidden), F32),
+        vmem((nz, nx * cap, hidden), BF16),
+        vmem((2, nz, nx, cap, wa), BF16),
+        vmem((2, nz, nx, cap, wb), BF16),
+        vmem((2, nz - 1, nx, cap, wa), BF16),
+        vmem((2, nx - 1, cap, wa), BF16),
+        vmem((2, nx - 1, nz, cap, wb), BF16),
+        vmem((2, nz - 1, cap, wb), BF16),
+        vmem((ne, cap, chunk), BF16),
+        vmem((ne, cap, chunk), BF16),
+        dma((3,)),
+        dma((ne,)),
+        dma((ne,)),
+        dma((2, nz, nx)),
+        dma((2, nz, nx)),
+        dma((2, nz - 1, nx)),
+        dma((2, nx - 1)),
+        dma((2, nx - 1, nz)),
+        dma((2, nz - 1)),
+        dma((ne,)),
+        dma((ne,)),
+    ] + [dma((2,))] * 8
+    return pl.pallas_call(
+        functools.partial(expert_kernel, (nz, nx, ne, cap, wa, wb)),
+        out_shape=jax.ShapeDtypeStruct(mixed.shape, BF16),
+        in_specs=[pl.BlockSpec(memory_space=pltpu.VMEM)] * 4 + [pl.BlockSpec(memory_space=pl.ANY)] * 3,
+        out_specs=pl.BlockSpec(memory_space=pltpu.VMEM),
+        scratch_shapes=scratch,
+        compiler_params=pltpu.CompilerParams(
+            collective_id=1, has_side_effects=True, vmem_limit_bytes=60 * 1024 * 1024
+        ),
+    )(mixed, place, wmap, gain, w_gate, w_up, w_down)
+
+
+def slot_keys(routes, expert_count, capacity):
+    tokens = routes.shape[0]
+    hot = (routes[:, :, None] == jnp.arange(expert_count, dtype=jnp.int32)).astype(F32)
+    before = (jnp.arange(tokens)[:, None] > jnp.arange(tokens)[None, :]).astype(F32)
+    earlier = jnp.dot(before, jnp.sum(hot, axis=1))
+    slot = jnp.sum(hot * earlier[:, None, :], axis=2).astype(jnp.int32)
+    return routes * capacity + slot
+
+
+def slot_maps(routes, gate_weights, expert_count, capacity):
+    keys = slot_keys(routes, expert_count, capacity)
+    rows = jnp.arange(expert_count * capacity, dtype=jnp.int32)
+    place = ((keys[None, :, 0] == rows[:, None]) | (keys[None, :, 1] == rows[:, None])).astype(BF16)
+    wmap = sum(jnp.where(keys[:, k, None] == rows[None, :], gate_weights[:, k, None], 0.0) for k in range(2))
+    return place, wmap
 
 
 def on_device(
@@ -153,41 +499,10 @@
     mixed = (residual.astype(jnp.float32) + query_short * conv.astype(jnp.float32)).astype(
         jnp.bfloat16
     )
-    local_experts = w_gate.shape[0]
-    expert_count = local_experts * exp_total
     topk_count = routes.shape[1]
-    capacity = 5 * row_count * topk_count // (4 * expert_count)
-    expert_hot = (routes[:, :, None] == jnp.arange(expert_count, dtype=jnp.int32)).astype(jnp.int32)
-    per_token = jnp.sum(expert_hot, axis=1)
-    earlier = jnp.cumsum(per_token, axis=0) - per_token
-    slot_index = jnp.sum(expert_hot * earlier[:, None, :], axis=2)
-    slot_hot = (slot_index[:, :, None] == jnp.arange(capacity, dtype=jnp.int32)).astype(jnp.float32)
-    hot_float = expert_hot.astype(jnp.float32)
-    placement_map = jnp.einsum("tke,tkc->ect", hot_float, slot_hot)
-    weight_map = jnp.einsum(
-        "tke,tkc,tk->ect", hot_float, slot_hot, gate_weights, precision=lax.Precision.HIGHEST
-    )
-    outgoing = jnp.einsum(
-        "ect,td->ecd", placement_map.astype(jnp.bfloat16), mixed, preferred_element_type=jnp.float32
-    ).astype(jnp.bfloat16)
-    arrived = lax.all_to_all(outgoing, "exp", split_axis=0, concat_axis=2, tiled=True)
-    normed = rms_rows(lax.all_gather(arrived, "seq", axis=1, tiled=True), norm_gain)
-    gate_act = jnp.einsum("end,edf->nef", normed, w_gate, preferred_element_type=jnp.float32)
-    up_act = jnp.einsum("end,edf->nef", normed, w_up, preferred_element_type=jnp.float32)
-    hidden = (jax.nn.silu(gate_act) * up_act).astype(jnp.bfloat16)
-    summed = lax.psum_scatter(
-        jnp.einsum("nef,efd->ned", hidden, w_down, preferred_element_type=jnp.float32).astype(
-            jnp.bfloat16
-        ),
-        "seq",
-        scatter_dimension=0,
-        tiled=True,
-    )
-    returned = lax.all_to_all(summed, "exp", split_axis=2, concat_axis=1, tiled=True)
-    combined = jnp.einsum(
-        "ect,ced->td", weight_map, returned.astype(jnp.float32), precision=lax.Precision.HIGHEST
-    )
-    return (mixed.astype(jnp.float32) + combined).astype(jnp.bfloat16)
+    capacity = 5 * row_count * topk_count // (4 * exp_total)
+    place, wmap = slot_maps(routes, gate_weights, exp_total, capacity)
+    return experts(mixed, place, wmap, norm_gain[None, :], w_gate, w_up, w_down, seq_total // 4, 4, (768, 1280))
 
 
 def solution(mesh):

time: 541 us -> 227 us (0.42)
  waiting for transfers between devices: 350 us -> 10.7 us
  Pallas kernels: 0 us -> 151 us
  matrix products: 45.5 us -> 12.4 us
  other arithmetic: 40.7 us -> 7.91 us
  blocking collectives: 16 us -> 0 us
  local copies, waits for them, and re-layouts: 31.9 us -> 16.2 us
  between operations: 13.9 us -> 0.27 us
  starting transfers between devices: 37.1 us -> 27.5 us
    reduce_scatter x1 -> x0, waiting for transfers between devices: 228 us -> none  [on_device(): lax.psum_scatter(jnp.einsum('nef,efd->ned', hidden, w_down, preferred_ele...]
    pallas_call x0 -> x1, Pallas kernels: none -> 151 us  [experts(): pl.pallas_call(functools.partial(expert_kernel, (nz, nx, ne, cap, wa, wb)...]
    all_gather x1 -> x0, waiting for transfers between devices: 102 us -> none  [on_device(): lax.all_gather(arrived, 'seq', axis=1, tiled=True)]
    dot_general x6 -> x1, matrix products: 33.2 us -> 0.13 us  [slot_keys(): earlier = jnp.dot(before, jnp.sum(hot, axis=1))]
    unnamed x2 -> x1, other arithmetic: 24.5 us -> 0.07 us
    all_to_all x1 -> x0, blocking collectives: 16 us -> none  [on_device(): lax.all_to_all(outgoing, 'exp', split_axis=0, concat_axis=2, tiled=True)]
    all_to_all x1, waiting for transfers between devices: 0.01 us -> 9.33 us  [on_device(): lax.all_to_all(value_proj, 'seq', split_axis=1, concat_axis=0, tiled=True)]
    all_to_all x1 -> x0, starting transfers between devices: 8.97 us -> none  [on_device(): lax.all_to_all(summed, 'exp', split_axis=2, concat_axis=1, tiled=True)]
  transfers between devices with their start and end apart: 7 -> 4, of which waited for: 5 -> 3; matrix products, arithmetic and copies ran while one was open for 6% -> 15% of each run, Pallas kernels for 0% -> 0%
where the time goes in v1:
time: 227 us; the launch traced here: 226 us
  Pallas kernels  151 us (67%)
  starting transfers between devices  27.5 us (12%)
  local copies, waits for them, and re-layouts  16.2 us (7%)
  matrix products  12.4 us (5%)
  waiting for transfers between devices  10.7 us (5%)
  other arithmetic  7.91 us (3%)
    pallas_call x1, Pallas kernels, experts(): pl.pallas_call(functools.partial(expert_kernel, (nz, nx, ne, cap, wa, wb)...  151 us
    unnamed x13, local copies, waits for them, and re-layouts  12.8 us
    all_to_all x1, starting transfers between devices, on_device(): lax.all_to_all(key_proj, 'seq', split_axis=1, concat_axis=0, tiled=True)  10.7 us
    all_to_all x1, waiting for transfers between devices, on_device(): lax.all_to_all(value_proj, 'seq', split_axis=1, concat_axis=0, tiled=True)  9.33 us
    all_to_all x1, starting transfers between devices, on_device(): lax.all_to_all(value_proj, 'seq', split_axis=1, concat_axis=0, tiled=True)  8.94 us
  transfers between devices with their start and end apart: 4, of which 3 were waited for; matrix products, arithmetic and copies ran while one was open for 15% of the time, Pallas kernels for 0%

profile of v1, /device:TPU:1, one launch (start us, length us, event | category | flops | bytes accessed | tf_op | source)
XLA Modules:
  0.0 225.9 jit_solution(7906703911798583246)
XLA Ops:
  0.0 0.7 slice.147
  0.7 3.9 %collective-permute-start = (bf16[1,2,512]{2,1,0:T(2,128)(2,1)S(1)}, bf16[1,2,512]{2,1,0:T(2,128)(2,1)S(1)}, u32[]{:S(2)}, u32[]{:S(2)}) collective-permute-start(bf16[1,2,512]{2,1,0:T(2,128)(2,1)S(1)} %slice.147), channel_id=1, source_target_pairs={{0,8},{8,16},{16,24},{24,32},{32,40},{40,48},{48,56},{56,64},{64,7... | collective-permute-start | bytes 6152 | tf_op jit(solution)/shard_map/ppermute | solution.py:18
  4.6 1.7 copy.48
  6.3 10.7 %all-to-all-start = ((bf16[128,32,16]{0,2,1:T(8,128)(2,1)}), bf16[128,32,16]{0,2,1:T(8,128)(2,1)S(1)}, u32[]{:S(2)}, u32[]{:S(2)}) async-start(bf16[128,32,16]{0,2,1:T(8,128)(2,1)} %bitcast.8), calls=%async_computation | async-start | bytes 262144 | tf_op jit(solution)/shard_map/all_to_all | solution.py:484
  17.1 0.1 broadcast_multiply_fusion.1
  17.2 0.1 broadcast_multiply_fusion
  17.4 0.7 negate_bitcast_fusion
  18.1 0.8 slice_bitcast_fusion.4
  18.8 0.7 convert_reduce_fusion
  19.5 0.1 fusion.53
  19.6 0.7 select_reduce_fusion
  20.4 0.7 convert_add_fusion
  21.1 0.7 fusion.35.place_ref
  21.7 1.1 fusion.29
  22.8 0.9 dynamic-slice_bitcast_fusion.5
  23.7 1.7 copy.50
  25.4 0.8 select_add_fusion.wmap_ref
  26.2 0.3 all-to-all-done
  26.5 8.9 %all-to-all-start.1 = ((bf16[128,32,16]{0,2,1:T(8,128)(2,1)}), bf16[128,32,16]{0,2,1:T(8,128)(2,1)S(1)}, u32[]{:S(2)}, u32[]{:S(2)}) async-start(bf16[128,32,16]{0,2,1:T(8,128)(2,1)} %bitcast.13), calls=%async_computation.1 | async-start | bytes 262144 | tf_op jit(solution)/shard_map/all_to_all | solution.py:485
  35.4 9.3 %all-to-all-done.1 = bf16[128,32,16]{0,2,1:T(8,128)(2,1)S(1)} async-done(((bf16[128,32,16]{0,2,1:T(8,128)(2,1)}), bf16[128,32,16]{0,2,1:T(8,128)(2,1)S(1)}, u32[]{:S(2)}, u32[]{:S(2)}) %all-to-all-start.1) | async-done | bytes 131104 | tf_op jit(solution)/shard_map/all_to_all | solution.py:485
  44.8 0.1 pad_convert_fusion
  44.9 0.4 convert_bitcast_fusion
  45.3 0.1 fusion.3
  45.4 0.2 copy.59
  45.5 1.2 convolution_bitcast_fusion
  46.7 1.2 convolution_bitcast_fusion.1
  47.9 1.2 fusion.12
  49.1 1.2 fusion.11
  50.4 1.2 convolution_subtract_fusion
  51.6 1.2 convolution_add_fusion
  52.8 0.2 multiply_subtract_fusion.1
  53.1 0.8 fusion.46
  53.9 0.8 fusion.44
  54.7 0.8 fusion.2
  55.6 0.8 fusion.1
  56.4 1.0 fusion.7
  57.4 0.8 fusion
  58.2 0.3 copy.65
  58.5 0.7 copy_bitcast_fusion.3
  59.2 3.9 %all-to-all-start.2 = ((bf16[32,128,16]{1,2,0:T(8,128)(2,1)}), bf16[32,128,16]{1,2,0:T(8,128)(2,1)S(1)}, u32[]{:S(2)}, u32[]{:S(2)}) async-start(bf16[32,128,16]{1,2,0:T(8,128)(2,1)} %copy_bitcast_fusion.3), calls=%async_computation.2 | async-start | bytes 262144 | tf_op jit(solution)/shard_map/all_to_all | solution.py:498
  63.0 0.8 fusion.136
  63.9 2.8 %copy.54.wg_hbm = bf16[1,4096,344]{2,1,0:T(8,128)(2,1)} copy(bf16[1,4096,344]{1,2,0:T(8,128)(2,1)S(1)} %copy-done) | data formatting | bytes 5636096 | tf_op args[10]
  66.7 4.6 %copy.55.wu_hbm = bf16[1,4096,344]{2,1,0:T(8,128)(2,1)} copy(bf16[1,4096,344]{1,2,0:T(8,128)(2,1)} %param.24) | data formatting | bytes 5636096 | tf_op args[11]
  71.3 1.1 all-to-all-done.2
  72.5 0.1 copy.53
  72.6 0.8 fusion.24.mixed_ref
  73.4 151.0 %shard_map.127 = bf16[128,512]{1,0:T(8,128)(2,1)} custom-call(bf16[128,512]{1,0:T(8,128)(2,1)} %fusion.24.mixed_ref, bf16[320,128]{1,0:T(8,128)(2,1)} %fusion.35.place_ref, f32[128,320]{1,0:T(8,128)} %select_add_fusion.wmap_ref, f32[1,4096]{1,0:T(1,128)} %bitcast.142, bf16[1,4096,344]{2,1,0:T(8,128)(2,1)} %copy.54.wg_hbm, ...), custom_call_target="tpu_custom_call" | custom-call | tf_op jit(solution)/shard_map/pallas_call | solution.py:429
  224.3 1.6 copy.67
  (13 shorter events, 0.1 us)
Async XLA Ops:
  0.7 70.6 %collective-permute-start = (bf16[1,2,512]{2,1,0:T(2,128)(2,1)S(1)}, bf16[1,2,512]{2,1,0:T(2,128)(2,1)S(1)}, u32[]{:S(2)}, u32[]{:S(2)}) collective-permute-start(bf16[1,2,512]{2,1,0:T(2,128)(2,1)S(1)} %slice.147), channel_id=1, source_target_pairs={{0,8},{8,16},{16,24},{24,32},{32,40},{40,48},{48,56},{56,64},{64,7... | collective-permute-start | bytes 6152 | tf_op jit(solution)/shard_map/ppermute | solution.py:18
  6.3 20.2 %all-to-all-start = ((bf16[128,32,16]{0,2,1:T(8,128)(2,1)}), bf16[128,32,16]{0,2,1:T(8,128)(2,1)S(1)}, u32[]{:S(2)}, u32[]{:S(2)}) async-start(bf16[128,32,16]{0,2,1:T(8,128)(2,1)} %bitcast.8), calls=%async_computation | async-start | bytes 262144 | tf_op jit(solution)/shard_map/all_to_all | solution.py:484
  26.5 18.3 %all-to-all-start.1 = ((bf16[128,32,16]{0,2,1:T(8,128)(2,1)}), bf16[128,32,16]{0,2,1:T(8,128)(2,1)S(1)}, u32[]{:S(2)}, u32[]{:S(2)}) async-start(bf16[128,32,16]{0,2,1:T(8,128)(2,1)} %bitcast.13), calls=%async_computation.1 | async-start | bytes 262144 | tf_op jit(solution)/shard_map/all_to_all | solution.py:485
  56.4 7.5 %copy-start = (bf16[1,4096,344]{1,2,0:T(8,128)(2,1)S(1)}, bf16[1,4096,344]{1,2,0:T(8,128)(2,1)}, u32[]{:S(2)}) copy-start(bf16[1,4096,344]{1,2,0:T(8,128)(2,1)} %param.23) | copy-start | bytes 8454148
  59.2 13.3 %all-to-all-start.2 = ((bf16[32,128,16]{1,2,0:T(8,128)(2,1)}), bf16[32,128,16]{1,2,0:T(8,128)(2,1)S(1)}, u32[]{:S(2)}, u32[]{:S(2)}) async-start(bf16[32,128,16]{1,2,0:T(8,128)(2,1)} %copy_bitcast_fusion.3), calls=%async_computation.2 | async-start | bytes 262144 | tf_op jit(solution)/shard_map/all_to_all | solution.py:498
  66.7 4.6 %copy-start.1 = (bf16[128,512]{1,0:T(8,128)(2,1)S(1)}, bf16[128,512]{1,0:T(8,128)(2,1)}, u32[]{:S(2)}) copy-start(bf16[128,512]{1,0:T(8,128)(2,1)} %param.14) | copy-start | bytes 393220
  66.7 6.0 %copy-start.2 = (bf16[128,512]{1,0:T(8,128)(2,1)S(1)}, bf16[128,512]{1,0:T(8,128)(2,1)}, u32[]{:S(2)}) copy-start(bf16[128,512]{1,0:T(8,128)(2,1)} %param.13) | copy-start | bytes 393220

commit v2 on v1

--- a/solution.py
+++ b/solution.py
@@ -1,5 +1,4 @@
 import functools
-import math
 
 import jax
 import jax.numpy as jnp
@@ -12,101 +11,144 @@
 F32, BF16 = jnp.float32, jnp.bfloat16
 
 
-def passed_along(value, axis, by):
-    devices = lax.axis_size(axis)
-    pairs = [(i, i + by) for i in range(devices) if 0 <= i + by < devices]
-    return lax.ppermute(value, axis, pairs)
-
-
-def short_filter(extended, kernel, length):
-    tap_count = kernel.shape[0]
-    signal = extended.astype(jnp.float32)
-    running = kernel[0] * signal[tap_count - 1 : tap_count - 1 + length]
-    for offset in range(1, tap_count):
-        running = (
-            running
-            + kernel[offset] * signal[tap_count - 1 - offset : tap_count - 1 - offset + length]
+def mixer_kernel(
+    dims,
+    res_ref, q_ref, k_ref, v_ref, filt_ref, raw_ref, decay_ref, root_ref, out_ref,
+    ext, rims, edge, taps, toep, zsend, zrecv, zrows, zpad, crows, csend, crecv,
+    rim_send, rim_recv, z_send, z_recv, c_send, c_recv,
+):
+    ns, tok, chans, tap_count = dims
+    length = ns * tok
+    s, e = lax.axis_index("seq"), lax.axis_index("exp")
+    rim = rims.shape[1]
+
+    def peer(i):
+        return (s + i) % ns
+
+    def remote(src, dst, send, recv, to):
+        return pltpu.make_async_remote_copy(
+            src_ref=src, dst_ref=dst, send_sem=send, recv_sem=recv, device_id=(to, e), device_id_type=MESH
         )
-    return running
-
-
-def with_zeros(signal, tap_count):
-    return jnp.concatenate(
-        (jnp.zeros((tap_count - 1, signal.shape[1]), signal.dtype), signal), axis=0
-    )
-
-
-def long_filter(raw_taps, decay_rate, length):
-    positions = jnp.arange(length).astype(jnp.float32)[:, None]
-    energy = jnp.expm1(-2.0 * decay_rate * length) / jnp.expm1(-2.0 * decay_rate)
-    return raw_taps * jnp.exp(-decay_rate * positions) / jnp.sqrt(energy)
-
-
-def angle_table(row_total, col_total, period):
-    product = (
-        jnp.arange(row_total, dtype=jnp.int32)[:, None]
-        * jnp.arange(col_total, dtype=jnp.int32)[None, :]
-        % period
-    )
-    theta = product.astype(jnp.float32) * (2.0 * math.pi / period)
-    return (jnp.cos(theta), jnp.sin(theta))
-
-
-def left_real(tables, direction, real_part):
-    cosine, sine = tables
-    highest = lax.Precision.HIGHEST
-    cos_real = jnp.einsum("kn,cnm->ckm", cosine, real_part, precision=highest)
-    sin_real = jnp.einsum("kn,cnm->ckm", sine, real_part, precision=highest)
-    return (cos_real, -direction * sin_real)
-
-
-def left_real_out(tables, direction, real_part, imag_part):
-    cosine, sine = tables
-    highest = lax.Precision.HIGHEST
-    cos_real = jnp.einsum("kn,cnm->ckm", cosine, real_part, precision=highest)
-    sin_imag = jnp.einsum("kn,cnm->ckm", sine, imag_part, precision=highest)
-    return cos_real + direction * sin_imag
-
-
-def right_apply(tables, direction, real_part, imag_part):
-    cosine, sine = tables
-    highest = lax.Precision.HIGHEST
-    cos_real = jnp.einsum("ckn,nm->ckm", real_part, cosine, precision=highest)
-    cos_imag = jnp.einsum("ckn,nm->ckm", imag_part, cosine, precision=highest)
-    sin_real = jnp.einsum("ckn,nm->ckm", real_part, sine, precision=highest)
-    sin_imag = jnp.einsum("ckn,nm->ckm", imag_part, sine, precision=highest)
-    return (cos_real + direction * sin_imag, cos_imag - direction * sin_real)
-
-
-def twist(tables, direction, real_part, imag_part):
-    cosine, sine = tables
-    return (
-        real_part * cosine + direction * imag_part * sine,
-        imag_part * cosine - direction * real_part * sine,
-    )
-
-
-def causal_conv(signal, taps):
-    channel_count, length = signal.shape
-    padded_size = 2 * length
-    second = 128
-    first = padded_size // second
-    first_tab = angle_table(first, first, first)
-    second_tab = angle_table(second, second, second)
-    twist_tab = angle_table(first, second, padded_size)
-    both = jnp.concatenate((signal, taps), axis=0)
-    real_part = jnp.pad(both, ((0, 0), (0, length))).reshape(2 * channel_count, first, second)
-    real_part, imag_part = left_real(first_tab, 1.0, real_part)
-    real_part, imag_part = twist(twist_tab, 1.0, real_part, imag_part)
-    real_part, imag_part = right_apply(second_tab, 1.0, real_part, imag_part)
-    sig_real, tap_real = (real_part[:channel_count], real_part[channel_count:])
-    sig_imag, tap_imag = (imag_part[:channel_count], imag_part[channel_count:])
-    prod_real = sig_real * tap_real - sig_imag * tap_imag
-    prod_imag = sig_real * tap_imag + sig_imag * tap_real
-    real_part, imag_part = right_apply(second_tab, -1.0, prod_real, prod_imag)
-    real_part, imag_part = twist(twist_tab, -1.0, real_part, imag_part)
-    real_part = left_real_out(first_tab, -1.0, real_part, imag_part)
-    return real_part.reshape(channel_count, padded_size)[:, :length] / padded_size
+
+    barrier = pltpu.get_barrier_semaphore()
+
+    def greet(i, carry):
+        pl.semaphore_signal(barrier, inc=1, device_id=(peer(i), e), device_id_type=MESH)
+        return carry
+
+    lax.fori_loop(1, ns, greet, 0)
+
+    for j, ref in enumerate((q_ref, k_ref, v_ref)):
+        edge[j] = ref[tok - rim :, :]
+        ext[j, 8 : 8 + tok] = ref[...].astype(F32)
+    zpad[...] = jnp.zeros_like(zpad)
+    position = lax.broadcasted_iota(jnp.int32, (chans, length), 1).astype(F32)
+    scaled = raw_ref[...] * jnp.exp(-decay_ref[...] * position) / root_ref[...]
+    for c in range(chans):
+        taps[c] = jnp.broadcast_to(scaled[c : c + 1, :], (8, length))
+
+    band = lax.broadcasted_iota(jnp.int32, (tok, tok), 1) >= lax.broadcasted_iota(jnp.int32, (tok, tok), 0)
+
+    def bands(c, carry):
+        before = jnp.zeros((tok, tok), F32)
+        for k in range(ns):
+            row = jnp.concatenate([taps[c, :, k * tok : (k + 1) * tok]] * (tok // 8), axis=0)
+            turned = pltpu.roll(row, 0, axis=1, stride=1, stride_axis=0)
+            full = jnp.where(band, turned, before)
+            high = full.astype(BF16)
+            toep[c, k * tok : (k + 1) * tok, :tok] = high
+            toep[c, k * tok : (k + 1) * tok, tok:] = (full - high.astype(F32)).astype(BF16)
+            before = turned
+        return carry
+
+    early = chans // 4
+    lax.fori_loop(0, early, bands, 0)
+    pl.semaphore_wait(barrier, ns - 1)
+
+    rim_copy = remote(edge, rims, rim_send, rim_recv, peer(1))
+    rim_copy.start()
+    lax.fori_loop(early, 2 * early, bands, 0)
+    rim_copy.wait()
+
+    def short(j):
+        return (
+            filt_ref[j, 0:1, :] * ext[j, 8 : 8 + tok]
+            + filt_ref[j, 1:2, :] * ext[j, 7 : 7 + tok]
+            + filt_ref[j, 2:3, :] * ext[j, 6 : 6 + tok]
+        )
+
+    for j in range(3):
+        ext[j, 0:8] = jnp.where(s == 0, 0.0, rims[j].astype(F32)[rim - 8 :])
+    zed = (short(1) * short(2)).astype(BF16).astype(F32)
+    zsend[...] = zed.T.astype(BF16).reshape(ns, chans, tok)
+    zrecv[s] = zsend[s]
+
+    def send_zed(i, carry):
+        remote(zsend.at[peer(i)], zrecv.at[s], z_send, z_recv, peer(i)).start()
+        return carry
+
+    lax.fori_loop(1, ns, send_zed, 0)
+    lax.fori_loop(2 * early, chans, bands, 0)
+    remote(zrecv.at[1:], zrecv.at[1:], z_recv, z_recv, peer(1)).wait_recv()
+
+    zrows[...] = zrecv[...].astype(F32).reshape(ns * chans, tok)
+
+    def convolve(c, carry):
+        zpad[c, ns:] = zrows[pl.ds(c, ns, stride=chans), :]
+        total = jnp.zeros((ns, 2 * tok), F32)
+        for k in range(0, ns, 2):
+            two = jnp.concatenate((zpad[c, ns - k : 2 * ns - k], zpad[c, ns - k - 1 : 2 * ns - k - 1]), axis=1).astype(BF16)
+            total += jnp.dot(two, toep[c, k * tok : (k + 2) * tok, :], preferred_element_type=F32)
+        crows[pl.ds(c, ns, stride=chans), :] = total[:, :tok] + total[:, tok:]
+        return carry
+
+    lax.fori_loop(0, chans, convolve, 0)
+    csend[...] = crows[...].astype(BF16).reshape(ns, chans, tok)
+    crecv[s] = csend[s]
+
+    def send_conv(i, carry):
+        remote(csend.at[peer(i)], crecv.at[s], c_send, c_recv, peer(i)).start()
+        return carry
+
+    lax.fori_loop(1, ns, send_conv, 0)
+    ext[1, 0:tok] = short(0)
+    remote(zsend.at[1:], zsend.at[1:], z_send, z_send, peer(1)).wait_send()
+    remote(crecv.at[1:], crecv.at[1:], c_recv, c_recv, peer(1)).wait_recv()
+    conv = crecv[...].astype(F32).reshape(ns * chans, tok).T
+    out_ref[...] = (res_ref[...].astype(F32) + ext[1, 0:tok] * conv).astype(BF16)
+    remote(csend.at[1:], csend.at[1:], c_send, c_send, peer(1)).wait_send()
+
+
+def mixer(residual, query, key, value, short_kernel, raw, decay):
+    ns = lax.axis_size("seq")
+    tok, width = query.shape
+    tap_count = short_kernel.shape[1]
+    chans, length = raw.shape
+    root = jnp.sqrt(jnp.expm1(-2.0 * decay * length) / jnp.expm1(-2.0 * decay))
+    vmem, dma = pltpu.VMEM, pltpu.SemaphoreType.DMA
+    return pl.pallas_call(
+        functools.partial(mixer_kernel, (ns, tok, chans, tap_count)),
+        out_shape=jax.ShapeDtypeStruct((tok, width), BF16),
+        in_specs=[pl.BlockSpec(memory_space=pltpu.VMEM)] * 8,
+        out_specs=pl.BlockSpec(memory_space=pltpu.VMEM),
+        scratch_shapes=[
+            vmem((3, 8 + tok, width), F32),
+            vmem((3, 16, width), BF16),
+            vmem((3, 16, width), BF16),
+            vmem((chans, 8, length), F32),
+            vmem((chans, length, 2 * tok), BF16),
+            vmem((ns, chans, tok), BF16),
+            vmem((ns, chans, tok), BF16),
+            vmem((ns * chans, tok), F32),
+            vmem((chans, 2 * ns, tok), F32),
+            vmem((ns * chans, tok), F32),
+            vmem((ns, chans, tok), BF16),
+            vmem((ns, chans, tok), BF16),
+        ] + [pltpu.SemaphoreType.DMA] * 6,
+        compiler_params=pltpu.CompilerParams(
+            collective_id=0, has_side_effects=True, vmem_limit_bytes=56 * 1024 * 1024
+        ),
+    )(residual, query, key, value, short_kernel, raw, decay, root)
 
 
 def expert_kernel(
@@ -208,15 +250,16 @@
     def group(d, t):
         return (nz - t) % nz if d else t
 
+    def across(rows, w):
+        return lax.dot_general(rows, w, (((1,), (1,)), ((), ())), preferred_element_type=F32)
+
     def project(d, t):
         at = group(d, t)
         left, right = rows_of(xa, d, t), rows_of(xb, d, t)
         one = slice(d * wa, (d + 1) * wa)
         two = slice(2 * wa + d * wb, 2 * wa + (d + 1) * wb)
         for total, w in ((acc_g, wg), (acc_u, wu)):
-            total[at] += jnp.dot(left, w[one, :], preferred_element_type=F32) + jnp.dot(
-                right, w[two, :], preferred_element_type=F32
-            )
+            total[at] += across(left, w[:, one]) + across(right, w[:, two])
 
     def activate(d, t):
         at = group(d, t)
@@ -396,8 +439,8 @@
     hidden = w_gate.shape[2]
     vmem, dma = pltpu.VMEM, pltpu.SemaphoreType.DMA
     scratch = [
-        vmem((width, hidden), BF16),
-        vmem((width, hidden), BF16),
+        vmem((hidden, width), BF16),
+        vmem((hidden, width), BF16),
         vmem((hidden, width), BF16),
         vmem((ne, cap, chunk), BF16),
         vmem((ne, cap, chunk), BF16),
@@ -435,7 +478,7 @@
         compiler_params=pltpu.CompilerParams(
             collective_id=1, has_side_effects=True, vmem_limit_bytes=60 * 1024 * 1024
         ),
-    )(mixed, place, wmap, gain, w_gate, w_up, w_down)
+    )(mixed, place, wmap, gain, jnp.swapaxes(w_gate, 1, 2), jnp.swapaxes(w_up, 1, 2), w_down)
 
 
 def slot_keys(routes, expert_count, capacity):
@@ -470,39 +513,21 @@
     w_up,
     w_down,
 ):
-    row_count, width_here = query_proj.shape
-    tap_count = short_kernel.shape[1]
-    seq_total = lax.axis_size("seq")
-    exp_total = lax.axis_size("exp")
-    length = row_count * seq_total
-    slice_width = width_here // seq_total
-    stacked = query_proj[None]
-    rims = passed_along(stacked[:, row_count - (tap_count - 1) :], "seq", 1)
-    extended = jnp.concatenate((rims, stacked), axis=1)
-    query_short = short_filter(extended[0], short_kernel[0], row_count)
-    key_full, value_full = (
-        lax.all_to_all(key_proj, "seq", split_axis=1, concat_axis=0, tiled=True),
-        lax.all_to_all(value_proj, "seq", split_axis=1, concat_axis=0, tiled=True),
+    tokens = query_proj.shape[0]
+    nz, nx = lax.axis_size("seq") // 4, 4
+    mixed = mixer(
+        residual,
+        query_proj,
+        key_proj,
+        value_proj,
+        short_kernel,
+        filter_raw[:, 0, :].T,
+        filter_decay.T,
     )
-    kernel_here = lax.dynamic_slice_in_dim(
-        short_kernel, lax.axis_index("seq") * slice_width, slice_width, 2
-    )
-    key_short = short_filter(with_zeros(key_full, tap_count), kernel_here[1], length)
-    value_short = short_filter(with_zeros(value_full, tap_count), kernel_here[2], length)
-    zed = (key_short * value_short).astype(jnp.bfloat16)
-    taps = long_filter(
-        filter_raw.reshape(length, slice_width), filter_decay.reshape(slice_width), length
-    )
-    conv_cols = causal_conv(zed.astype(jnp.float32).T, taps.T)
-    conv_here = conv_cols.T.astype(jnp.bfloat16)
-    conv = lax.all_to_all(conv_here, "seq", split_axis=0, concat_axis=1, tiled=True)
-    mixed = (residual.astype(jnp.float32) + query_short * conv.astype(jnp.float32)).astype(
-        jnp.bfloat16
-    )
-    topk_count = routes.shape[1]
-    capacity = 5 * row_count * topk_count // (4 * exp_total)
-    place, wmap = slot_maps(routes, gate_weights, exp_total, capacity)
-    return experts(mixed, place, wmap, norm_gain[None, :], w_gate, w_up, w_down, seq_total // 4, 4, (768, 1280))
+    expert_total = lax.axis_size("exp")
+    capacity = 5 * tokens * routes.shape[1] // (4 * expert_total)
+    place, wmap = slot_maps(routes, gate_weights, expert_total, capacity)
+    return experts(mixed, place, wmap, norm_gain[None, :], w_gate, w_up, w_down, nz, nx, (768, 1280))
 
 
 def solution(mesh):

time: 227 us -> 193 us (0.85)
  Pallas kernels: 151 us -> 186 us
  starting transfers between devices: 27.5 us -> 0 us
  local copies, waits for them, and re-layouts: 16.2 us -> 3.07 us
  matrix products: 12.4 us -> 0.13 us
  waiting for transfers between devices: 10.7 us -> 0 us
  other arithmetic: 7.91 us -> 4.17 us
    pallas_call x0 -> x1, Pallas kernels: none -> 34.2 us  [mixer(): pl.pallas_call(functools.partial(mixer_kernel, (ns, tok, chans, tap_count...]
    all_to_all x3 -> x0, starting transfers between devices: 23.5 us -> none  [the longest x1 10.7 us: on_device(): lax.all_to_all(key_proj, 'seq', split_axis=1, concat_axis=0, tiled=True)]
    dot_general x12 -> x0, matrix products: 12.3 us -> none  [the longest x2 2.05 us: right_apply(): sin_real = jnp.einsum('ckn,nm->ckm', real_part, sine, precision=highest)]
    unnamed x13 -> x3, local copies, waits for them, and re-layouts: 12.8 us -> 1.57 us
    all_to_all x3 -> x0, waiting for transfers between devices: 10.7 us -> none  [the longest x1 9.33 us: on_device(): lax.all_to_all(value_proj, 'seq', split_axis=1, concat_axis=0, tiled=True)]
    ppermute x1 -> x0, starting transfers between devices: 3.93 us -> none  [passed_along(): return lax.ppermute(value, axis, pairs)]
  transfers between devices with their start and end apart: 4 -> 0, of which waited for: 3 -> 0; matrix products, arithmetic and copies ran while one was open for 15% -> 0% of each run, Pallas kernels for 0% -> 0%
where the time goes in v2:
time: 193 us
  Pallas kernels  186 us (96%)
  other arithmetic  4.17 us (2%)
  local copies, waits for them, and re-layouts  3.07 us (2%)
    pallas_call x1, Pallas kernels, experts(): pl.pallas_call(functools.partial(expert_kernel, (nz, nx, ne, cap, wa, wb)...  152 us
    pallas_call x1, Pallas kernels, mixer(): pl.pallas_call(functools.partial(mixer_kernel, (ns, tok, chans, tap_count...  34.2 us

profile of v2, /device:TPU:1, one launch (start us, length us, event | category | flops | bytes accessed | tf_op | source)
XLA Modules:
  0.0 193.3 jit_solution(11054092817590311074)
XLA Ops:
  0.0 0.8 slice_bitcast_fusion.1
  0.8 0.7 convert_reduce_fusion
  1.4 0.1 fusion.2
  1.6 0.7 select_reduce_fusion
  2.3 0.7 convert_add_fusion
  3.0 0.7 copy.25.decay_ref
  3.7 0.0 copy-start
  3.7 0.6 divide_sqrt_fusion.root_ref
  4.3 0.7 fusion.1.place_ref
  5.0 0.0 copy-done
  5.0 34.2 %shard_map.127.mixed_ref = bf16[128,512]{1,0:T(8,128)(2,1)} custom-call(bf16[128,512]{1,0:T(8,128)(2,1)} %res_ref.1, bf16[128,512]{1,0:T(8,128)(2,1)} %q_ref.1, bf16[128,512]{1,0:T(8,128)(2,1)} %k_ref.1, bf16[128,512]{1,0:T(8,128)(2,1)} %v_ref.1, f32[3,3,512]{2,1,0:T(4,128)} %filt_ref.1, f32[16,4096]{1,0:T(8,128)} %bitcast.18, f32[16,1]{1,0:T(8,128)} %copy-done, ...), custom_call_target="tpu_custom_call" | custom-call | tf_op jit(solution)/shard_map/pallas_call | solution.py:129
  39.2 0.8 select_add_fusion.wmap_ref
  40.0 151.6 %shard_map.128 = bf16[128,512]{1,0:T(8,128)(2,1)} custom-call(bf16[128,512]{1,0:T(8,128)(2,1)} %shard_map.127.mixed_ref, bf16[320,128]{1,0:T(8,128)(2,1)} %fusion.1.place_ref, f32[128,320]{1,0:T(8,128)} %select_add_fusion.wmap_ref, f32[1,4096]{1,0:T(1,128)} %bitcast.19, bf16[1,344,4096]{2,1,0:T(8,128)(2,1)} %bitcast.16, bf16[1,344,4096]{2,1,0:T(8,128)(2,1)} %bitcast.17, ...), custom_call_target="tpu_custom_call" | custom-call | tf_op jit(solution)/shard_map/pallas_call | solution.py:472
  191.7 1.6 copy.27
  (1 shorter events, 0.0 us)
Async XLA Ops:
  3.7 1.3 copy-start

commit v3 on v0

v3 whole, which is shorter than its diff:
```python
import functools

import jax
import jax.numpy as jnp
from jax import lax
from jax.experimental import pallas as pl
from jax.experimental.pallas import tpu as pltpu
from jax.sharding import PartitionSpec as P

MESH = pl.DeviceIdType.MESH
F32, BF16 = jnp.float32, jnp.bfloat16


def column(row):
    n = row.shape[1]
    same = lax.broadcasted_iota(jnp.int32, (n, n), 0) == lax.broadcasted_iota(jnp.int32, (n, n), 1)
    return jnp.sum(jnp.where(same, jnp.broadcast_to(row, (n, n)), 0.0), axis=1, keepdims=True)


def less_one(v):
    series = jnp.ones_like(v)
    for n in range(11, 1, -1):
        series = 1.0 + v * (1.0 / n) * series
    return jnp.where(v > -0.5, v * series, jnp.exp(v) - 1.0)


def slot_maps(routes_ref, picks_ref, place, wmap, ne, cap):
    topk, tok = routes_ref.shape
    routes = routes_ref[...]
    ids = lax.broadcasted_iota(jnp.int32, (ne, tok), 0)
    hot = [(ids == routes[k : k + 1]).astype(F32) for k in range(topk)]
    before = lax.broadcasted_iota(jnp.int32, (tok, tok), 0) < lax.broadcasted_iota(jnp.int32, (tok, tok), 1)
    earlier = jnp.dot(sum(hot).astype(BF16), before.astype(F32).astype(BF16), preferred_element_type=F32)
    row = lax.broadcasted_iota(jnp.int32, (ne * cap, tok), 0).astype(F32)
    marks, weights = 0.0, 0.0
    for k in range(topk):
        key = routes[k : k + 1].astype(F32) * cap + jnp.sum(hot[k] * earlier, axis=0, keepdims=True)
        marks += jnp.where(row == key, 1.0, 0.0)
        weights += jnp.where(row == key, picks_ref[k : k + 1, :], 0.0)
    place[...] = marks.astype(BF16)
    wmap[...] = weights


def block_kernel(
    dims,
    res_ref, q_ref, k_ref, v_ref, filt_ref, raw_ref, decay_ref, routes_ref, picks_ref, gain_ref, wg_hbm, wu_hbm, wd_hbm,
    out_ref,
    mixed, place, wmap, ext, rims, edge, zsend, zrecv, csend, crecv,
    wg, wu, wd, outg, arr, xa, xb, rc1, rc2, rd1, rd2, yb, ret,
    rim_send, rim_recv, z_send, z_recv, c_send, c_recv,
    w_sem, go_send, go_recv, a_recv, b_recv, rc1_recv, rc2_recv, rd1_recv, rd2_recv, back_send, back_recv,
    az_send, ax_send, bz_send, bx_send, cz_send, cx_send, dz_send, dx_send,
):
    nz, nx, ne, cap, wa, wb = dims
    width = 2 * (wa + wb)
    chunk = width // ne
    ns, tok = nz * nx, q_ref.shape[0]
    chans, length = raw_ref.shape
    rim = rims.shape[1]
    s, e = lax.axis_index("seq"), lax.axis_index("exp")
    z, x = s // nx, s % nx

    def peer(i):
        return (s + i) % ns

    def along_z(d):
        return (((z + (1, nz - 1)[d]) % nz) * nx + x, e)

    def along_x(d):
        return (z * nx + (x + (1, nx - 1)[d]) % nx, e)

    def expert(i):
        return (s, (e + i) % ne)

    def remote(src, dst, send, recv, to):
        return pltpu.make_async_remote_copy(
            src_ref=src, dst_ref=dst, send_sem=send, recv_sem=recv, device_id=to, device_id_type=MESH
        )

    def arrived(dst, recv):
        remote(dst, dst, recv, recv, along_z(0)).wait_recv()

    def sent(src, send):
        remote(src, src, send, send, along_z(0)).wait_send()

    weights = [
        pltpu.make_async_copy(h.at[0], v, w_sem.at[i]) for i, (h, v) in enumerate(((wg_hbm, wg), (wu_hbm, wu), (wd_hbm, wd)))
    ]
    for copy in weights:
        copy.start()

    barrier = pltpu.get_barrier_semaphore()

    def greet(i, carry):
        pl.semaphore_signal(barrier, inc=1, device_id=(peer(i), e), device_id_type=MESH)
        return carry

    lax.fori_loop(1, ns, greet, 0)
    for i in range(1, ne):
        pl.semaphore_signal(barrier, inc=1, device_id=expert(i), device_id_type=MESH)

    def mixer(taps, toep, zrows, zpad, crows):
        for j, ref in enumerate((q_ref, k_ref, v_ref)):
            edge[j] = ref[tok - rim :, :]
            ext[j, 8 : 8 + tok] = ref[...].astype(F32)
        zpad[...] = jnp.zeros_like(zpad)
        position = lax.broadcasted_iota(jnp.int32, (chans, length), 1).astype(F32)
        decay = column(decay_ref[...])
        root = jnp.sqrt(less_one(-2.0 * decay * length) / less_one(-2.0 * decay))
        scaled = raw_ref[...] * jnp.exp(-decay * position) / root
        for c in range(chans):
            taps[c] = jnp.broadcast_to(scaled[c : c + 1, :], (8, length))

        band = lax.broadcasted_iota(jnp.int32, (tok, tok), 1) >= lax.broadcasted_iota(jnp.int32, (tok, tok), 0)

        def bands(c, carry):
            before = jnp.zeros((tok, tok), F32)
            for k in range(ns):
                row = jnp.concatenate([taps[c, :, k * tok : (k + 1) * tok]] * (tok // 8), axis=0)
                turned = pltpu.roll(row, 0, axis=1, stride=1, stride_axis=0)
                full = jnp.where(band, turned, before)
                toep[c, k * tok : (k + 1) * tok, :] = full.astype(BF16)
                before = turned
            return carry

        early = chans // 4
        lax.fori_loop(0, early, bands, 0)
        slot_maps(routes_ref, picks_ref, place, wmap, ne, cap)
        pl.semaphore_wait(barrier, ns - 1 + ne - 1)

        rim_copy = remote(edge, rims, rim_send, rim_recv, (peer(1), e))
        rim_copy.start()
        lax.fori_loop(early, 2 * early, bands, 0)
        rim_copy.wait()

        def short(j):
            return (
                filt_ref[j, 0:1, :] * ext[j, 8 : 8 + tok]
                + filt_ref[j, 1:2, :] * ext[j, 7 : 7 + tok]
                + filt_ref[j, 2:3, :] * ext[j, 6 : 6 + tok]
            )

        for j in range(3):
            ext[j, 0:8] = jnp.where(s == 0, 0.0, rims[j].astype(F32)[rim - 8 :])
        zed = (short(1) * short(2)).astype(BF16).astype(F32)
        zsend[...] = zed.T.astype(BF16).reshape(ns, chans, tok)
        zrecv[s] = zsend[s]

        def send_zed(i, carry):
            remote(zsend.at[peer(i)], zrecv.at[s], z_send, z_recv, (peer(i), e)).start()
            return carry

        lax.fori_loop(1, ns, send_zed, 0)
        lax.fori_loop(2 * early, chans, bands, 0)
        remote(zrecv.at[1:], zrecv.at[1:], z_recv, z_recv, (peer(1), e)).wait_recv()

        zrows[...] = zrecv[...].astype(F32).reshape(ns * chans, tok)

        def convolve(c):
            zpad[c, ns:] = zrows[pl.ds(c, ns, stride=chans), :]
            total = jnp.zeros((ns, tok), F32)
            for k in range(0, ns, 2):
                two = jnp.concatenate((zpad[c, ns - k : 2 * ns - k], zpad[c, ns - k - 1 : 2 * ns - k - 1]), axis=1).astype(BF16)
                total += jnp.dot(two, toep[c, k * tok : (k + 2) * tok, :], preferred_element_type=F32)
            crows[pl.ds(c, ns, stride=chans), :] = total

        def convolve_some(g, carry):
            for c in range(chans // 4):
                convolve(g * (chans // 4) + c)
            return carry

        lax.fori_loop(0, 4, convolve_some, 0)
        csend[...] = crows[...].astype(BF16).reshape(ns, chans, tok)
        crecv[s] = csend[s]

        def send_conv(i, carry):
            remote(csend.at[peer(i)], crecv.at[s], c_send, c_recv, (peer(i), e)).start()
            return carry

        lax.fori_loop(1, ns, send_conv, 0)
        ext[1, 0:tok] = short(0)
        remote(zsend.at[1:], zsend.at[1:], z_send, z_send, (peer(1), e)).wait_send()
        remote(crecv.at[1:], crecv.at[1:], c_recv, c_recv, (peer(1), e)).wait_recv()
        conv = crecv[...].astype(F32).reshape(ns * chans, tok).T
        mixed[...] = (res_ref[...].astype(F32) + ext[1, 0:tok] * conv).astype(BF16)
        remote(csend.at[1:], csend.at[1:], c_send, c_send, (peer(1), e)).wait_send()

    vmem = pltpu.VMEM
    pl.run_scoped(
        mixer,
        vmem((chans, 8, length), F32),
        vmem((chans, length, tok), BF16),
        vmem((ns * chans, tok), F32),
        vmem((chans, 2 * ns, tok), F32),
        vmem((ns * chans, tok), F32),
    )

    def experts(acc_g, acc_u, hid, pc, pd):
        picked = jnp.dot(place[...], mixed[...], preferred_element_type=F32)
        outg[...] = picked.reshape(ne, cap, chunk).astype(BF16)
        arr[e] = outg[e]
        for i in range(1, ne):
            remote(outg.at[(e + i) % ne], arr.at[e], go_send.at[i], go_recv.at[i], expert(i)).start()
        acc_g[...] = jnp.zeros_like(acc_g)
        acc_u[...] = jnp.zeros_like(acc_u)
        for i in range(1, ne):
            arrived(arr.at[(e + ne - i) % ne], go_recv.at[i])
        square = jnp.zeros((cap, 1), F32)
        for c in range(ne):
            values = arr[c].astype(F32)
            square += jnp.sum(values * values, axis=-1, keepdims=True)
        scale = lax.rsqrt(square / width + 1e-06)
        spans = []
        for d in range(2):
            spans.append((xa, pc, d, d * wa, wa))
            spans.append((xb, pd, d, 2 * wa + d * wb, wb))
        for c in range(ne):
            values = (arr[c].astype(F32) * scale * gain_ref[:, c * chunk : (c + 1) * chunk]).astype(BF16)
            for ref, _, d, start, size in spans:
                lo, hi = max(start, c * chunk), min(start + size, (c + 1) * chunk)
                if lo < hi:
                    ref[d, 0, 0, :, lo - start : hi - start] = values[:, lo - c * chunk : hi - c * chunk]

        def a_along_z(d, t, j):
            remote(xa.at[d, t, j], xa.at[d, t + 1, j], az_send.at[d], a_recv.at[d, t + 1, j], along_z(d)).start()

        def a_along_x(d, j):
            remote(xa.at[d, 0, j], xa.at[d, 0, j + 1], ax_send.at[d], a_recv.at[d, 0, j + 1], along_x(d)).start()

        def b_along_z(d, t):
            remote(xb.at[d, t, 0], xb.at[d, t + 1, 0], bz_send.at[d], b_recv.at[d, t + 1, 0], along_z(d)).start()

        def b_along_x(d, t, j):
            remote(xb.at[d, t, j], xb.at[d, t, j + 1], bx_send.at[d], b_recv.at[d, t, j + 1], along_x(d)).start()

        for d in range(2):
            b_along_z(d, 0)
            a_along_x(d, 0)
        for d in range(2):
            b_along_x(d, 0, 0)
            a_along_z(d, 0, 0)

        def turned(j, d):
            return (nx - j) % nx if d else j

        def rows_of(ref, d, t):
            parts = [ref[d, t, turned(j, d)].astype(F32) for j in range(nx)]
            return jnp.concatenate(parts, axis=0).astype(BF16)

        def group(d, t):
            return (nz - t) % nz if d else t

        def across(rows, w):
            return lax.dot_general(rows, w, (((1,), (1,)), ((), ())), preferred_element_type=F32)

        def project(d, t):
            at = group(d, t)
            left, right = rows_of(xa, d, t), rows_of(xb, d, t)
            one = slice(d * wa, (d + 1) * wa)
            two = slice(2 * wa + d * wb, 2 * wa + (d + 1) * wb)
            for total, w in ((acc_g, wg), (acc_u, wu)):
                total[at] += across(left, w[:, one]) + across(right, w[:, two])

        def activate(d, t):
            at = group(d, t)
            gate = acc_g[at]
            hid[at] = (gate / (1.0 + jnp.exp(-gate)) * acc_u[at]).astype(BF16)

        def gather_step(p, carry):
            for d in range(2):
                @pl.when(p <= nz - 1)
                def _():
                    arrived(xb.at[d, p, 0], b_recv.at[d, p, 0])
                    b_along_x(d, p, 0)

                @pl.when(p < nz - 1)
                def _():
                    b_along_z(d, p)

                @pl.when(p <= nx - 1)
                def _():
                    arrived(xa.at[d, 0, p], a_recv.at[d, 0, p])
                    a_along_z(d, 0, p)

                @pl.when(p < nx - 1)
                def _():
                    a_along_x(d, p)

            for j in range(nx):
                for d in range(2):
                    t = p - j

                    @pl.when((t >= 1) & (t <= nz - 1))
                    def _():
                        arrived(xa.at[d, t, j], a_recv.at[d, t, j])

                    @pl.when((t >= 1) & (t < nz - 1))
                    def _():
                        a_along_z(d, t, j)

                if j >= 1:
                    for d in range(2):
                        t = p - j

                        @pl.when((t >= 0) & (t <= nz - 1))
                        def _():
                            arrived(xb.at[d, t, j], b_recv.at[d, t, j])
                            if j < nx - 1:
                                b_along_x(d, t, j)

            @pl.when(p == nx - 1)
            def _():
                for copy in weights:
                    copy.wait()

            for d in range(2):
                t = p - (nx - 1)

                @pl.when(t >= 0)
                def _():
                    project(d, t)

                @pl.when((t > nz // 2) | ((t == 0) | (t == nz // 2)) & (d == 1))
                def _():
                    activate(d, t)

            return carry

        lax.fori_loop(1, nz + nx - 1, gather_step, 0)

        def down(d, q):
            at = group(d, q % nz)
            rows = hid[at]
            for ref, start, size in ((pc, d * wa, wa), (pd, 2 * wa + d * wb, wb)):
                part = jnp.dot(rows, wd[:, start : start + size], preferred_element_type=F32)
                for j in range(nx):
                    ref[d, q - 1, turned(j, d)] = part[j * cap : (j + 1) * cap].astype(BF16)

        def add(total, more):
            total[...] = (total[...].astype(F32) + more[...].astype(F32)).astype(BF16)

        for d in range(2):
            down(d, 1)

        def reduce_step(p, carry):
            for d in range(2):
                for v in range(1, nx + 1):
                    k, j = p - v + 1, v % nx

                    @pl.when((k >= 1) & (k <= nz))
                    def _():
                        if v >= 2:
                            arrived(rd1.at[d, v - 2, k - 1], rd1_recv.at[d, v - 2, k - 1])
                            add(pd.at[d, k - 1, j], rd1.at[d, v - 2, k - 1])
                        if v < nx:
                            remote(
                                pd.at[d, k - 1, j], rd1.at[d, v - 1, k - 1], dx_send.at[d], rd1_recv.at[d, v - 1, k - 1], along_x(d)
                            ).start()
                        else:
                            @pl.when(k >= 2)
                            def _():
                                arrived(rd2.at[d, k - 2], rd2_recv.at[d, k - 2])
                                add(pd.at[d, k - 1, 0], rd2.at[d, k - 2])

                            @pl.when(k < nz)
                            def _():
                                remote(
                                    pd.at[d, k - 1, 0], rd2.at[d, k - 1], dz_send.at[d], rd2_recv.at[d, k - 1], along_z(d)
                                ).start()

            for d in range(2):
                for v in range(1, nx + 1):
                    q, j = p - v + 1, v % nx

                    @pl.when((q >= 2) & (q <= nz))
                    def _():
                        arrived(rc1.at[d, q - 2, j], rc1_recv.at[d, q - 2, j])
                        add(pc.at[d, q - 1, j], rc1.at[d, q - 2, j])

                    @pl.when((q >= 1) & (q < nz))
                    def _():
                        remote(
                            pc.at[d, q - 1, j], rc1.at[d, q - 1, j], cz_send.at[d], rc1_recv.at[d, q - 1, j], along_z(d)
                        ).start()

                    @pl.when(q == nz)
                    def _():
                        if v >= 2:
                            arrived(rc2.at[d, v - 2], rc2_recv.at[d, v - 2])
                            add(pc.at[d, nz - 1, j], rc2.at[d, v - 2])
                        if v < nx:
                            remote(
                                pc.at[d, nz - 1, j], rc2.at[d, v - 1], cx_send.at[d], rc2_recv.at[d, v - 1], along_x(d)
                            ).start()

            for d in range(2):
                @pl.when(p < nz)
                def _():
                    down(d, p + 1)

            return carry

        lax.fori_loop(1, nz + nx, reduce_step, 0)

        for c in range(ne):
            for _, ref, d, start, size in spans:
                lo, hi = max(start, c * chunk), min(start + size, (c + 1) * chunk)
                if lo < hi:
                    yb[c, :, lo - c * chunk : hi - c * chunk] = ref[d, nz - 1, 0, :, lo - start : hi - start]
        for i in range(1, ne):
            remote(yb.at[(e + i) % ne], ret.at[e], back_send.at[i], back_recv.at[i], expert(i)).start()
        ret[e] = yb[e]
        for d in range(2):
            sent(xa.at[d, 0 : nz - 1], az_send.at[d])
            sent(xa.at[d, 0, 0 : nx - 1], ax_send.at[d])
            sent(xb.at[d, 0 : nz - 1, 0], bz_send.at[d])
            sent(xb.at[d, :, 0 : nx - 1], bx_send.at[d])
            sent(pc.at[d, 0 : nz - 1], cz_send.at[d])
            sent(pc.at[d, nz - 1, 0 : nx - 1], cx_send.at[d])
            sent(pd.at[d, 0 : nz - 1, 0], dz_send.at[d])
            sent(pd.at[d, :, 0 : nx - 1], dx_send.at[d])
        for i in range(1, ne):
            sent(outg.at[i], go_send.at[i])
        for i in range(1, ne):
            arrived(ret.at[(e + ne - i) % ne], back_recv.at[i])
        rows = ret[...].astype(F32).reshape(ne * cap, chunk)
        combined = lax.dot_general(
            wmap[...], rows, (((0,), (0,)), ((), ())), preferred_element_type=F32, precision=lax.Precision.HIGHEST
        )
        out_ref[...] = (mixed[...].astype(F32) + combined).astype(BF16)
        for i in range(1, ne):
            sent(yb.at[i], back_send.at[i])

    hidden = wd.shape[0]
    pl.run_scoped(
        experts,
        vmem((nz, nx * cap, hidden), F32),
        vmem((nz, nx * cap, hidden), F32),
        vmem((nz, nx * cap, hidden), BF16),
        vmem((2, nz, nx, cap, wa), BF16),
        vmem((2, nz, nx, cap, wb), BF16),
    )


def block(residual, query, key, value, short_kernel, raw, decay, routes, picks, gain, w_gate, w_up, w_down, nz, nx, parts):
    ns, ne = nz * nx, lax.axis_size("exp")
    tok, chunk = query.shape
    chans, length = raw.shape
    cap = 5 * tok * routes.shape[0] // (4 * ne)
    width = ne * chunk
    wa, wb = parts
    hidden = w_gate.shape[1]
    vmem, dma = pltpu.VMEM, pltpu.SemaphoreType.DMA
    scratch = [
        vmem((tok, chunk), BF16),
        vmem((ne * cap, tok), BF16),
        vmem((ne * cap, tok), F32),
        vmem((3, 8 + tok, chunk), F32),
        vmem((3, 16, chunk), BF16),
        vmem((3, 16, chunk), BF16),
    ]
    scratch += [vmem((ns, chans, tok), BF16)] * 4
    scratch += [vmem((hidden, width), BF16)] * 3
    scratch += [
        vmem((ne, cap, chunk), BF16),
        vmem((ne, cap, chunk), BF16),
        vmem((2, nz, nx, cap, wa), BF16),
        vmem((2, nz, nx, cap, wb), BF16),
        vmem((2, nz - 1, nx, cap, wa), BF16),
        vmem((2, nx - 1, cap, wa), BF16),
        vmem((2, nx - 1, nz, cap, wb), BF16),
        vmem((2, nz - 1, cap, wb), BF16),
        vmem((ne, cap, chunk), BF16),
        vmem((ne, cap, chunk), BF16),
    ]
    scratch += [dma] * 6
    scratch += [
        dma((3,)),
        dma((ne,)),
        dma((ne,)),
        dma((2, nz, nx)),
        dma((2, nz, nx)),
        dma((2, nz - 1, nx)),
        dma((2, nx - 1)),
        dma((2, nx - 1, nz)),
        dma((2, nz - 1)),
        dma((ne,)),
        dma((ne,)),
    ] + [dma((2,))] * 8
    return pl.pallas_call(
        functools.partial(block_kernel, (nz, nx, ne, cap, wa, wb)),
        out_shape=jax.ShapeDtypeStruct((tok, chunk), BF16),
        in_specs=[pl.BlockSpec(memory_space=pltpu.VMEM)] * 10 + [pl.BlockSpec(memory_space=pl.ANY)] * 3,
        out_specs=pl.BlockSpec(memory_space=pltpu.VMEM),
        scratch_shapes=scratch,
        compiler_params=pltpu.CompilerParams(
            collective_id=0, has_side_effects=True, vmem_limit_bytes=61 * 1024 * 1024
        ),
    )(residual, query, key, value, short_kernel, raw, decay, routes, picks, gain, w_gate, w_up, w_down)


def on_device(
    residual,
    query_proj,
    key_proj,
    value_proj,
    short_kernel,
    filter_raw,
    filter_decay,
    routes,
    gate_weights,
    norm_gain,
    w_gate,
    w_up,
    w_down,
):
    return block(
        residual,
        query_proj,
        key_proj,
        value_proj,
        short_kernel,
        filter_raw[:, 0, :].T,
        filter_decay,
        routes.T,
        gate_weights.T,
        norm_gain[None, :],
        jnp.swapaxes(w_gate, 1, 2),
        jnp.swapaxes(w_up, 1, 2),
        w_down,
        lax.axis_size("seq") // 4,
        4,
        (768, 1280),
    )


def solution(mesh):
    in_specs = (
        P("seq", "exp"),
        P("seq", "exp"),
        P("seq", "exp"),
        P("seq", "exp"),
        P(None, None, "exp"),
        P(None, "exp", "seq"),
        P("exp", "seq"),
        P("seq", None),
        P("seq", None),
        P(),
        P("exp", None, "seq"),
        P("exp", None, "seq"),
        P("exp", "seq", None),
    )
    out_specs = P("seq", "exp")
    return jax.shard_map(
        on_device, mesh=mesh, in_specs=in_specs, out_specs=out_specs, check_vma=False
    )
```

time: 541 us -> 178 us (0.33); the launches traced: 535 us -> 178 us
  waiting for transfers between devices: 350 us -> 0 us
  Pallas kernels: 0 us -> 176 us
  matrix products: 45.5 us -> 0 us
  other arithmetic: 40.7 us -> 0 us
  starting transfers between devices: 37.1 us -> 0 us
  local copies, waits for them, and re-layouts: 31.9 us -> 1.57 us
  blocking collectives: 16 us -> 0 us
  between operations: 13.9 us -> 0.01 us
    reduce_scatter x1 -> x0, waiting for transfers between devices: 228 us -> none  [on_device(): lax.psum_scatter(jnp.einsum('nef,efd->ned', hidden, w_down, preferred_ele...]
    pallas_call x0 -> x1, Pallas kernels: none -> 176 us  [block(): pl.pallas_call(functools.partial(block_kernel, (nz, nx, ne, cap, wa, wb))...]
    all_gather x1 -> x0, waiting for transfers between devices: 102 us -> none  [on_device(): lax.all_gather(arrived, 'seq', axis=1, tiled=True)]
    dot_general x18 -> x0, matrix products: 45.5 us -> none  [the longest x1 20 us: on_device(): jnp.einsum('nef,efd->ned', hidden, w_down, preferred_element_type=jnp.flo...]
    all_to_all x4 -> x0, starting transfers between devices: 33.3 us -> none  [the longest x1 11.9 us: on_device(): lax.all_to_all(value_proj, 'seq', split_axis=1, concat_axis=0, tiled=True)]
    unnamed x2 -> x0, other arithmetic: 24.5 us -> none
    all_to_all x4 -> x0, waiting for transfers between devices: 20.4 us -> none  [the longest x1 9.14 us: on_device(): lax.all_to_all(key_proj, 'seq', split_axis=1, concat_axis=0, tiled=True)]
    all_to_all x1 -> x0, blocking collectives: 16 us -> none  [on_device(): lax.all_to_all(outgoing, 'exp', split_axis=0, concat_axis=2, tiled=True)]
  transfers between devices with their start and end apart: 7 -> 0, of which waited for: 5 -> 0; matrix products, arithmetic and copies ran while one was open for 6% -> 0% of each run, Pallas kernels for 0% -> 0%
where the time goes in v3:
time: 178 us
  Pallas kernels  176 us (99%)
    pallas_call x1, Pallas kernels, block(): pl.pallas_call(functools.partial(block_kernel, (nz, nx, ne, cap, wa, wb))...  176 us

profile of v3, /device:TPU:1, one launch (start us, length us, event | category | flops | bytes accessed | tf_op | source)
XLA Modules:
  0.0 178.0 jit_solution(8671644768849913451)
XLA Ops:
  0.0 176.4 %shard_map.127 = bf16[128,512]{1,0:T(8,128)(2,1)} custom-call(bf16[128,512]{1,0:T(8,128)(2,1)} %res_ref.1, bf16[128,512]{1,0:T(8,128)(2,1)} %q_ref.1, bf16[128,512]{1,0:T(8,128)(2,1)} %k_ref.1, bf16[128,512]{1,0:T(8,128)(2,1)} %v_ref.1, f32[3,3,512]{2,1,0:T(4,128)} %filt_ref.1, f32[16,4096]{1,0:T(8,128)} %bitcast.10, f32[1,16]{1,0:T(1,128)} %decay_ref.1, ...), custom_call_target="tpu_custom_call" | custom-call | tf_op jit(solution)/shard_map/pallas_call | solution.py:490
  176.4 1.6 copy.15

commit v4 on v3

--- a/solution.py
+++ b/solution.py
@@ -56,12 +56,22 @@
     chunk = width // ne
     ns, tok = nz * nx, q_ref.shape[0]
     chans, length = raw_ref.shape
-    rim = rims.shape[1]
     s, e = lax.axis_index("seq"), lax.axis_index("exp")
     z, x = s // nx, s % nx
 
     def peer(i):
-        return (s + i) % ns
+        return (z + i // nx) % nz * nx + (x + i % nx) % nx
+
+    def hops(i):
+        return min(i // nx, nz - i // nx) + min(i % nx, nx - i % nx)
+
+    far_first = sorted(range(1, ns), key=lambda i: -hops(i))
+    chips = ne // 2
+
+    def owner(i, way):
+        return (e // 2 + (i // 2 if way > 0 else chips - i // 2)) % chips * 2 + (e + i) % 2
+
+    experts_far_first = sorted(range(1, ne), key=lambda i: (-min(i // 2, chips - i // 2), i))
 
     def along_z(d):
         return (((z + (1, nz - 1)[d]) % nz) * nx + x, e)
@@ -70,7 +80,7 @@
         return (z * nx + (x + (1, nx - 1)[d]) % nx, e)
 
     def expert(i):
-        return (s, (e + i) % ne)
+        return (s, owner(i, 1))
 
     def remote(src, dst, send, recv, to):
         return pltpu.make_async_remote_copy(
@@ -101,7 +111,7 @@
 
     def mixer(taps, toep, zrows, zpad, crows):
         for j, ref in enumerate((q_ref, k_ref, v_ref)):
-            edge[j] = ref[tok - rim :, :]
+            edge[2 * j : 2 * j + 2] = ref[tok - 16 :, :].astype(F32)[14:]
             ext[j, 8 : 8 + tok] = ref[...].astype(F32)
         zpad[...] = jnp.zeros_like(zpad)
         position = lax.broadcasted_iota(jnp.int32, (chans, length), 1).astype(F32)
@@ -128,7 +138,8 @@
         slot_maps(routes_ref, picks_ref, place, wmap, ne, cap)
         pl.semaphore_wait(barrier, ns - 1 + ne - 1)
 
-        rim_copy = remote(edge, rims, rim_send, rim_recv, (peer(1), e))
+        edge[6:8] = jnp.zeros((2, edge.shape[1]), F32)
+        rim_copy = remote(edge, rims, rim_send, rim_recv, ((s + 1) % ns, e))
         rim_copy.start()
         lax.fori_loop(early, 2 * early, bands, 0)
         rim_copy.wait()
@@ -141,16 +152,13 @@
             )
 
         for j in range(3):
-            ext[j, 0:8] = jnp.where(s == 0, 0.0, rims[j].astype(F32)[rim - 8 :])
+            ext[j, 6:8] = jnp.where(s == 0, 0.0, rims[2 * j : 2 * j + 2])
         zed = (short(1) * short(2)).astype(BF16).astype(F32)
         zsend[...] = zed.T.astype(BF16).reshape(ns, chans, tok)
         zrecv[s] = zsend[s]
 
-        def send_zed(i, carry):
+        for i in far_first:
             remote(zsend.at[peer(i)], zrecv.at[s], z_send, z_recv, (peer(i), e)).start()
-            return carry
-
-        lax.fori_loop(1, ns, send_zed, 0)
         lax.fori_loop(2 * early, chans, bands, 0)
         remote(zrecv.at[1:], zrecv.at[1:], z_recv, z_recv, (peer(1), e)).wait_recv()
 
@@ -173,11 +181,8 @@
         csend[...] = crows[...].astype(BF16).reshape(ns, chans, tok)
         crecv[s] = csend[s]
 
-        def send_conv(i, carry):
+        for i in far_first:
             remote(csend.at[peer(i)], crecv.at[s], c_send, c_recv, (peer(i), e)).start()
-            return carry
-
-        lax.fori_loop(1, ns, send_conv, 0)
         ext[1, 0:tok] = short(0)
         remote(zsend.at[1:], zsend.at[1:], z_send, z_send, (peer(1), e)).wait_send()
         remote(crecv.at[1:], crecv.at[1:], c_recv, c_recv, (peer(1), e)).wait_recv()
@@ -198,18 +203,19 @@
     def experts(acc_g, acc_u, hid, pc, pd):
         picked = jnp.dot(place[...], mixed[...], preferred_element_type=F32)
         outg[...] = picked.reshape(ne, cap, chunk).astype(BF16)
+        for i in experts_far_first:
+            remote(outg.at[owner(i, 1)], arr.at[e], go_send.at[i], go_recv.at[i], expert(i)).start()
         arr[e] = outg[e]
-        for i in range(1, ne):
-            remote(outg.at[(e + i) % ne], arr.at[e], go_send.at[i], go_recv.at[i], expert(i)).start()
         acc_g[...] = jnp.zeros_like(acc_g)
         acc_u[...] = jnp.zeros_like(acc_u)
-        for i in range(1, ne):
-            arrived(arr.at[(e + ne - i) % ne], go_recv.at[i])
-        square = jnp.zeros((cap, 1), F32)
-        for c in range(ne):
-            values = arr[c].astype(F32)
-            square += jnp.sum(values * values, axis=-1, keepdims=True)
-        scale = lax.rsqrt(square / width + 1e-06)
+        own = outg[e].astype(F32)
+        squares = own * own
+        for i in reversed(experts_far_first):
+            source = owner(i, -1)
+            arrived(arr.at[source], go_recv.at[i])
+            values = arr[source].astype(F32)
+            squares += values * values
+        scale = lax.rsqrt(jnp.sum(squares, axis=-1, keepdims=True) / width + 1e-06)
         spans = []
         for d in range(2):
             spans.append((xa, pc, d, d * wa, wa))
@@ -316,11 +322,11 @@
             for d in range(2):
                 t = p - (nx - 1)
 
-                @pl.when(t >= 0)
+                @pl.when((t >= 0) & (t < nz - 1))
                 def _():
                     project(d, t)
 
-                @pl.when((t > nz // 2) | ((t == 0) | (t == nz // 2)) & (d == 1))
+                @pl.when((t > nz // 2) & (t < nz - 1) | ((t == 0) | (t == nz // 2)) & (d == 1))
                 def _():
                     activate(d, t)
 
@@ -339,60 +345,70 @@
         def add(total, more):
             total[...] = (total[...].astype(F32) + more[...].astype(F32)).astype(BF16)
 
+        def sum_wide(p, d):
+            for v in range(1, nx + 1):
+                k, j = p - v + 1, v % nx
+
+                @pl.when((k >= 1) & (k <= nz))
+                def _():
+                    if v >= 2:
+                        arrived(rd1.at[d, v - 2, k - 1], rd1_recv.at[d, v - 2, k - 1])
+                        add(pd.at[d, k - 1, j], rd1.at[d, v - 2, k - 1])
+                    if v < nx:
+                        remote(
+                            pd.at[d, k - 1, j], rd1.at[d, v - 1, k - 1], dx_send.at[d], rd1_recv.at[d, v - 1, k - 1], along_x(d)
+                        ).start()
+                    else:
+                        @pl.when(k >= 2)
+                        def _():
+                            arrived(rd2.at[d, k - 2], rd2_recv.at[d, k - 2])
+                            add(pd.at[d, k - 1, 0], rd2.at[d, k - 2])
+
+                        @pl.when(k < nz)
+                        def _():
+                            remote(
+                                pd.at[d, k - 1, 0], rd2.at[d, k - 1], dz_send.at[d], rd2_recv.at[d, k - 1], along_z(d)
+                            ).start()
+
+        def sum_narrow(p, d):
+            for v in range(1, nx + 1):
+                q, j = p - v + 1, v % nx
+
+                @pl.when((q >= 2) & (q <= nz))
+                def _():
+                    arrived(rc1.at[d, q - 2, j], rc1_recv.at[d, q - 2, j])
+                    add(pc.at[d, q - 1, j], rc1.at[d, q - 2, j])
+
+                @pl.when((q >= 1) & (q < nz))
+                def _():
+                    remote(
+                        pc.at[d, q - 1, j], rc1.at[d, q - 1, j], cz_send.at[d], rc1_recv.at[d, q - 1, j], along_z(d)
+                    ).start()
+
+                @pl.when(q == nz)
+                def _():
+                    if v >= 2:
+                        arrived(rc2.at[d, v - 2], rc2_recv.at[d, v - 2])
+                        add(pc.at[d, nz - 1, j], rc2.at[d, v - 2])
+                    if v < nx:
+                        remote(
+                            pc.at[d, nz - 1, j], rc2.at[d, v - 1], cx_send.at[d], rc2_recv.at[d, v - 1], along_x(d)
+                        ).start()
+
+        for d in (1, 0):
+            project(d, nz - 1)
+            activate(d, nz - 1)
+            down(1 - d, 1)
+            sum_wide(1, 1 - d)
+            sum_narrow(1, 1 - d)
         for d in range(2):
-            down(d, 1)
+            down(d, 2)
 
         def reduce_step(p, carry):
             for d in range(2):
-                for v in range(1, nx + 1):
-                    k, j = p - v + 1, v % nx
-
-                    @pl.when((k >= 1) & (k <= nz))
-                    def _():
-                        if v >= 2:
-                            arrived(rd1.at[d, v - 2, k - 1], rd1_recv.at[d, v - 2, k - 1])
-                            add(pd.at[d, k - 1, j], rd1.at[d, v - 2, k - 1])
-                        if v < nx:
-                            remote(
-                                pd.at[d, k - 1, j], rd1.at[d, v - 1, k - 1], dx_send.at[d], rd1_recv.at[d, v - 1, k - 1], along_x(d)
-                            ).start()
-                        else:
-                            @pl.when(k >= 2)
-                            def _():
-                                arrived(rd2.at[d, k - 2], rd2_recv.at[d, k - 2])
-                                add(pd.at[d, k - 1, 0], rd2.at[d, k - 2])
-
-                            @pl.when(k < nz)
-                            def _():
-                                remote(
-                                    pd.at[d, k - 1, 0], rd2.at[d, k - 1], dz_send.at[d], rd2_recv.at[d, k - 1], along_z(d)
-                                ).start()
-
+                sum_wide(p, d)
             for d in range(2):
-                for v in range(1, nx + 1):
-                    q, j = p - v + 1, v % nx
-
-                    @pl.when((q >= 2) & (q <= nz))
-                    def _():
-                        arrived(rc1.at[d, q - 2, j], rc1_recv.at[d, q - 2, j])
-                        add(pc.at[d, q - 1, j], rc1.at[d, q - 2, j])
-
-                    @pl.when((q >= 1) & (q < nz))
-                    def _():
-                        remote(
-                            pc.at[d, q - 1, j], rc1.at[d, q - 1, j], cz_send.at[d], rc1_recv.at[d, q - 1, j], along_z(d)
-                        ).start()
-
-                    @pl.when(q == nz)
-                    def _():
-                        if v >= 2:
-                            arrived(rc2.at[d, v - 2], rc2_recv.at[d, v - 2])
-                            add(pc.at[d, nz - 1, j], rc2.at[d, v - 2])
-                        if v < nx:
-                            remote(
-                                pc.at[d, nz - 1, j], rc2.at[d, v - 1], cx_send.at[d], rc2_recv.at[d, v - 1], along_x(d)
-                            ).start()
-
+                sum_narrow(p, d)
             for d in range(2):
                 @pl.when(p < nz)
                 def _():
@@ -400,15 +416,15 @@
 
             return carry
 
-        lax.fori_loop(1, nz + nx, reduce_step, 0)
+        lax.fori_loop(2, nz + nx, reduce_step, 0)
 
         for c in range(ne):
             for _, ref, d, start, size in spans:
                 lo, hi = max(start, c * chunk), min(start + size, (c + 1) * chunk)
                 if lo < hi:
                     yb[c, :, lo - c * chunk : hi - c * chunk] = ref[d, nz - 1, 0, :, lo - start : hi - start]
-        for i in range(1, ne):
-            remote(yb.at[(e + i) % ne], ret.at[e], back_send.at[i], back_recv.at[i], expert(i)).start()
+        for i in experts_far_first:
+            remote(yb.at[owner(i, 1)], ret.at[e], back_send.at[i], back_recv.at[i], expert(i)).start()
         ret[e] = yb[e]
         for d in range(2):
             sent(xa.at[d, 0 : nz - 1], az_send.at[d])
@@ -422,12 +438,12 @@
         for i in range(1, ne):
             sent(outg.at[i], go_send.at[i])
         for i in range(1, ne):
-            arrived(ret.at[(e + ne - i) % ne], back_recv.at[i])
+            arrived(ret.at[owner(i, -1)], back_recv.at[i])
         rows = ret[...].astype(F32).reshape(ne * cap, chunk)
         combined = lax.dot_general(
             wmap[...], rows, (((0,), (0,)), ((), ())), preferred_element_type=F32, precision=lax.Precision.HIGHEST
         )
-        out_ref[...] = (mixed[...].astype(F32) + combined).astype(BF16)
+        out_ref[...] = mixed[...].astype(F32) + combined
         for i in range(1, ne):
             sent(yb.at[i], back_send.at[i])
 
@@ -456,8 +472,8 @@
         vmem((ne * cap, tok), BF16),
         vmem((ne * cap, tok), F32),
         vmem((3, 8 + tok, chunk), F32),
-        vmem((3, 16, chunk), BF16),
-        vmem((3, 16, chunk), BF16),
+        vmem((8, chunk), F32),
+        vmem((8, chunk), F32),
     ]
     scratch += [vmem((ns, chans, tok), BF16)] * 4
     scratch += [vmem((hidden, width), BF16)] * 3
@@ -489,7 +505,7 @@
     ] + [dma((2,))] * 8
     return pl.pallas_call(
         functools.partial(block_kernel, (nz, nx, ne, cap, wa, wb)),
-        out_shape=jax.ShapeDtypeStruct((tok, chunk), BF16),
+        out_shape=jax.ShapeDtypeStruct((tok, chunk), F32),
         in_specs=[pl.BlockSpec(memory_space=pltpu.VMEM)] * 10 + [pl.BlockSpec(memory_space=pl.ANY)] * 3,
         out_specs=pl.BlockSpec(memory_space=pltpu.VMEM),
         scratch_shapes=scratch,
@@ -531,7 +547,7 @@
         lax.axis_size("seq") // 4,
         4,
         (768, 1280),
-    )
+    ).astype(BF16)
 
 
 def solution(mesh):

time: 178 us -> 176 us (0.989)
  Pallas kernels: 176 us -> 174 us
    pallas_call x1, Pallas kernels: 176 us -> 174 us  [block(): pl.pallas_call(functools.partial(block_kernel, (nz, nx, ne, cap, wa, wb))...]
where the time goes in v4:
time: 176 us; the launch traced here: 175 us
  Pallas kernels  174 us (99%)
    pallas_call x1, Pallas kernels, block(): pl.pallas_call(functools.partial(block_kernel, (nz, nx, ne, cap, wa, wb))...  174 us

profile of v4, /device:TPU:1, one launch (start us, length us, event | category | flops | bytes accessed | tf_op | source)
XLA Modules:
  0.0 175.4 jit_solution(15890701039718162664)
XLA Ops:
  0.0 173.8 %shard_map.127 = f32[128,512]{1,0:T(8,128)} custom-call(bf16[128,512]{1,0:T(8,128)(2,1)} %res_ref.1, bf16[128,512]{1,0:T(8,128)(2,1)} %q_ref.1, bf16[128,512]{1,0:T(8,128)(2,1)} %k_ref.1, bf16[128,512]{1,0:T(8,128)(2,1)} %v_ref.1, f32[3,3,512]{2,1,0:T(4,128)} %filt_ref.1, f32[16,4096]{1,0:T(8,128)} %bitcast.10, f32[1,16]{1,0:T(1,128)} %decay_ref.1, ...), custom_call_target="tpu_custom_call" | custom-call | tf_op jit(solution)/shard_map/pallas_call | solution.py:506
  173.8 1.6 convert_element_type.3

commit v5 on v4

--- a/solution.py
+++ b/solution.py
@@ -24,7 +24,7 @@
     return jnp.where(v > -0.5, v * series, jnp.exp(v) - 1.0)
 
 
-def slot_maps(routes_ref, picks_ref, place, wmap, ne, cap):
+def slot_maps(routes_ref, picks_ref, place, wmap, keys, ne, cap):
     topk, tok = routes_ref.shape
     routes = routes_ref[...]
     ids = lax.broadcasted_iota(jnp.int32, (ne, tok), 0)
@@ -33,8 +33,10 @@
     earlier = jnp.dot(sum(hot).astype(BF16), before.astype(F32).astype(BF16), preferred_element_type=F32)
     row = lax.broadcasted_iota(jnp.int32, (ne * cap, tok), 0).astype(F32)
     marks, weights = 0.0, 0.0
+    keys[...] = jnp.zeros_like(keys)
     for k in range(topk):
         key = routes[k : k + 1].astype(F32) * cap + jnp.sum(hot[k] * earlier, axis=0, keepdims=True)
+        keys[k : k + 1] = key
         marks += jnp.where(row == key, 1.0, 0.0)
         weights += jnp.where(row == key, picks_ref[k : k + 1, :], 0.0)
     place[...] = marks.astype(BF16)
@@ -46,14 +48,19 @@
     res_ref, q_ref, k_ref, v_ref, filt_ref, raw_ref, decay_ref, routes_ref, picks_ref, gain_ref, wg_hbm, wu_hbm, wd_hbm,
     out_ref,
     mixed, place, wmap, ext, rims, edge, zsend, zrecv, csend, crecv,
-    wg, wu, wd, outg, arr, xa, xb, rc1, rc2, rd1, rd2, yb, ret,
+    wg, wu, wd, gain, outg, arr, xa, xb, fr, fk, fs, xf, rc1, rc2, rd1, rd2, yb, ret,
     rim_send, rim_recv, z_send, z_recv, c_send, c_recv,
     w_sem, go_send, go_recv, a_recv, b_recv, rc1_recv, rc2_recv, rd1_recv, rd2_recv, back_send, back_recv,
     az_send, ax_send, bz_send, bx_send, cz_send, cx_send, dz_send, dx_send,
+    fr_recv, fk_recv, f_recv, f_send, fr_send, fk_send,
 ):
     nz, nx, ne, cap, wa, wb = dims
     width = 2 * (wa + wb)
     chunk = width // ne
+    few = chunk // 4
+    rest = chunk - few
+    ga = ne * rest * 5 // 24
+    gb = ne * rest // 2 - ga
     ns, tok = nz * nx, q_ref.shape[0]
     chans, length = raw_ref.shape
     s, e = lax.axis_index("seq"), lax.axis_index("exp")
@@ -93,11 +100,18 @@
     def sent(src, send):
         remote(src, src, send, send, along_z(0)).wait_send()
 
-    weights = [
-        pltpu.make_async_copy(h.at[0], v, w_sem.at[i]) for i, (h, v) in enumerate(((wg_hbm, wg), (wu_hbm, wu), (wd_hbm, wd)))
-    ]
-    for copy in weights:
-        copy.start()
+    columns = []
+    for c in range(ne):
+        columns.append((few * c, chunk * c, few))
+        columns.append((ne * few + rest * c, chunk * c + few, rest))
+    weights = [pltpu.make_async_copy(wd_hbm.at[0], wd, w_sem.at[2])]
+    weights[0].start()
+    for i, (h, v) in enumerate(((wg_hbm, wg), (wu_hbm, wu))):
+        for new, old, size in columns:
+            pltpu.make_async_copy(h.at[0, :, old : old + size], v.at[:, new : new + size], w_sem.at[i]).start()
+        weights.append(pltpu.make_async_copy(h.at[0], v, w_sem.at[i]))
+    for new, old, size in columns:
+        gain[:, new : new + size] = gain_ref[:, old : old + size]
 
     barrier = pltpu.get_barrier_semaphore()
 
@@ -135,7 +149,7 @@
 
         early = chans // 4
         lax.fori_loop(0, early, bands, 0)
-        slot_maps(routes_ref, picks_ref, place, wmap, ne, cap)
+        slot_maps(routes_ref, picks_ref, place, wmap, fk.at[0, 0], ne, cap)
         pl.semaphore_wait(barrier, ns - 1 + ne - 1)
 
         edge[6:8] = jnp.zeros((2, edge.shape[1]), F32)
@@ -200,32 +214,83 @@
         vmem((ns * chans, tok), F32),
     )
 
-    def experts(acc_g, acc_u, hid, pc, pd):
-        picked = jnp.dot(place[...], mixed[...], preferred_element_type=F32)
-        outg[...] = picked.reshape(ne, cap, chunk).astype(BF16)
+    def experts(acc_g, acc_u, acc_s, hid, pc, pd):
+        core = e % 2
+
+        def raw_along_z(t):
+            to = (z + 1 + core * (nz - 2)) % nz * nx + x
+            for ref, send, recv in ((fr, fr_send, fr_recv), (fk, fk_send, fk_recv)):
+                remote(ref.at[t, 0], ref.at[t + 1, 0], send.at[0], recv.at[t + 1, 0], (to, e)).start()
+
+        def raw_along_x(t, j):
+            to = z * nx + (x + 1 + core * (nx - 2)) % nx
+            for ref, send, recv in ((fr, fr_send, fr_recv), (fk, fk_send, fk_recv)):
+                remote(ref.at[t, j], ref.at[t, j + 1], send.at[1], recv.at[t, j + 1], (to, e)).start()
+
+        def spread(t, j):
+            keys = fk[t, j]
+            row = lax.broadcasted_iota(jnp.int32, (ne * cap, tok), 0).astype(F32)
+            marks = jnp.where((row == keys[0:1]) | (row == keys[1:2]), 1.0, 0.0).astype(BF16)
+            picked = jnp.dot(marks, fr[t, j], preferred_element_type=F32)
+            picked = picked.reshape(ne, cap, few).astype(BF16)
+            tz, jx = (t + core * (nz - 2 * t)) % nz, (j + core * (nx - 2 * j)) % nx
+            for c in range(ne):
+                fs[t, c, jx] = picked[c]
+            if j == nx - 1:
+                for i in experts_far_first:
+                    remote(fs.at[t, owner(i, 1)], xf.at[tz, e], f_send, f_recv.at[tz], expert(i)).start()
+                xf[tz, e] = fs[t, e]
+
+        def raw_step(h):
+            for j in range(nx):
+                t = h - j
+
+                @pl.when((t >= 0) & (t <= nz - 1))
+                def _():
+                    arrived(fr.at[t, j], fr_recv.at[t, j])
+                    arrived(fk.at[t, j], fk_recv.at[t, j])
+                    if j < nx - 1:
+                        raw_along_x(t, j)
+
+                if j == 0:
+                    @pl.when(t < nz - 1)
+                    def _():
+                        raw_along_z(t)
+
+        def spread_step(h):
+            for j in range(nx):
+                t = h - j
+
+                @pl.when((t >= 0) & (t <= nz - 1))
+                def _():
+                    spread(t, j)
+
+        fr[0, 0] = mixed[:, :few]
+        raw_along_z(0)
+        raw_along_x(0, 0)
+        picked = jnp.dot(place[...], mixed[:, few:], preferred_element_type=F32)
+        outg[...] = picked.reshape(ne, cap, rest).astype(BF16)
         for i in experts_far_first:
             remote(outg.at[owner(i, 1)], arr.at[e], go_send.at[i], go_recv.at[i], expert(i)).start()
         arr[e] = outg[e]
+        spread(0, 0)
+        raw_step(1)
         acc_g[...] = jnp.zeros_like(acc_g)
         acc_u[...] = jnp.zeros_like(acc_u)
-        own = outg[e].astype(F32)
-        squares = own * own
+        acc_s[...] = jnp.zeros_like(acc_s)
+        for h in range(2, nx):
+            raw_step(h)
         for i in reversed(experts_far_first):
-            source = owner(i, -1)
-            arrived(arr.at[source], go_recv.at[i])
-            values = arr[source].astype(F32)
-            squares += values * values
-        scale = lax.rsqrt(jnp.sum(squares, axis=-1, keepdims=True) / width + 1e-06)
+            arrived(arr.at[owner(i, -1)], go_recv.at[i])
+        for c in range(ne):
+            for ref, d, start, size in ((xa, 0, 0, ga), (xa, 1, ga, ga), (xb, 0, 2 * ga, gb), (xb, 1, 2 * ga + gb, gb)):
+                lo, hi = max(start, c * rest), min(start + size, (c + 1) * rest)
+                if lo < hi:
+                    ref[d, 0, 0, :, lo - start : hi - start] = arr[c, :, lo - c * rest : hi - c * rest]
         spans = []
         for d in range(2):
-            spans.append((xa, pc, d, d * wa, wa))
-            spans.append((xb, pd, d, 2 * wa + d * wb, wb))
-        for c in range(ne):
-            values = (arr[c].astype(F32) * scale * gain_ref[:, c * chunk : (c + 1) * chunk]).astype(BF16)
-            for ref, _, d, start, size in spans:
-                lo, hi = max(start, c * chunk), min(start + size, (c + 1) * chunk)
-                if lo < hi:
-                    ref[d, 0, 0, :, lo - start : hi - start] = values[:, lo - c * chunk : hi - c * chunk]
+            spans.append((pc, d, d * wa, wa))
+            spans.append((pd, d, 2 * wa + d * wb, wb))
 
         def a_along_z(d, t, j):
             remote(xa.at[d, t, j], xa.at[d, t + 1, j], az_send.at[d], a_recv.at[d, t + 1, j], along_z(d)).start()
@@ -245,13 +310,15 @@
         for d in range(2):
             b_along_x(d, 0, 0)
             a_along_z(d, 0, 0)
+        for h in range(1, nx):
+            spread_step(h)
 
         def turned(j, d):
             return (nx - j) % nx if d else j
 
         def rows_of(ref, d, t):
             parts = [ref[d, t, turned(j, d)].astype(F32) for j in range(nx)]
-            return jnp.concatenate(parts, axis=0).astype(BF16)
+            return jnp.concatenate(parts, axis=0)
 
         def group(d, t):
             return (nz - t) % nz if d else t
@@ -259,18 +326,26 @@
         def across(rows, w):
             return lax.dot_general(rows, w, (((1,), (1,)), ((), ())), preferred_element_type=F32)
 
+        def take(at, rows, start):
+            cols = slice(start, start + rows.shape[1])
+            acc_s[at] += jnp.sum(rows * rows, axis=-1, keepdims=True)
+            rows = (rows * gain[:, cols]).astype(BF16)
+            acc_g[at] += across(rows, wg[:, cols])
+            acc_u[at] += across(rows, wu[:, cols])
+
         def project(d, t):
             at = group(d, t)
-            left, right = rows_of(xa, d, t), rows_of(xb, d, t)
-            one = slice(d * wa, (d + 1) * wa)
-            two = slice(2 * wa + d * wb, 2 * wa + (d + 1) * wb)
-            for total, w in ((acc_g, wg), (acc_u, wu)):
-                total[at] += across(left, w[:, one]) + across(right, w[:, two])
+            take(at, rows_of(xa, d, t), ne * few + d * ga)
+            take(at, rows_of(xb, d, t), ne * few + 2 * ga + d * gb)
 
         def activate(d, t):
             at = group(d, t)
-            gate = acc_g[at]
-            hid[at] = (gate / (1.0 + jnp.exp(-gate)) * acc_u[at]).astype(BF16)
+            arrived(xf.at[at, 0 : ne - 1], f_recv.at[at])
+            rows = [jnp.concatenate([xf[at, c, j].astype(F32) for c in range(ne)], axis=1) for j in range(nx)]
+            take(at, jnp.concatenate(rows, axis=0), 0)
+            scale = lax.rsqrt(acc_s[at] / width + 1e-06)
+            gate = acc_g[at] * scale
+            hid[at] = (gate / (1.0 + jnp.exp(-gate)) * (acc_u[at] * scale)).astype(BF16)
 
         def gather_step(p, carry):
             for d in range(2):
@@ -313,6 +388,11 @@
                             arrived(xb.at[d, t, j], b_recv.at[d, t, j])
                             if j < nx - 1:
                                 b_along_x(d, t, j)
+
+            @pl.when(p <= nz - 1)
+            def _():
+                raw_step(p + nx - 1)
+                spread_step(p + nx - 1)
 
             @pl.when(p == nx - 1)
             def _():
@@ -419,7 +499,7 @@
         lax.fori_loop(2, nz + nx, reduce_step, 0)
 
         for c in range(ne):
-            for _, ref, d, start, size in spans:
+            for ref, d, start, size in spans:
                 lo, hi = max(start, c * chunk), min(start + size, (c + 1) * chunk)
                 if lo < hi:
                     yb[c, :, lo - c * chunk : hi - c * chunk] = ref[d, nz - 1, 0, :, lo - start : hi - start]
@@ -427,6 +507,11 @@
             remote(yb.at[owner(i, 1)], ret.at[e], back_send.at[i], back_recv.at[i], expert(i)).start()
         ret[e] = yb[e]
         for d in range(2):
+            for ref, send in ((fr, fr_send), (fk, fk_send)):
+                if d == 0:
+                    sent(ref.at[0 : nz - 1, 0], send.at[0])
+                else:
+                    sent(ref.at[:, 0 : nx - 1], send.at[1])
             sent(xa.at[d, 0 : nz - 1], az_send.at[d])
             sent(xa.at[d, 0, 0 : nx - 1], ax_send.at[d])
             sent(xb.at[d, 0 : nz - 1, 0], bz_send.at[d])
@@ -435,6 +520,7 @@
             sent(pc.at[d, nz - 1, 0 : nx - 1], cx_send.at[d])
             sent(pd.at[d, 0 : nz - 1, 0], dz_send.at[d])
             sent(pd.at[d, :, 0 : nx - 1], dx_send.at[d])
+        sent(fs.at[:, 0 : ne - 1], f_send)
         for i in range(1, ne):
             sent(outg.at[i], go_send.at[i])
         for i in range(1, ne):
@@ -452,6 +538,7 @@
         experts,
         vmem((nz, nx * cap, hidden), F32),
         vmem((nz, nx * cap, hidden), F32),
+        vmem((nz, nx * cap, 1), F32),
         vmem((nz, nx * cap, hidden), BF16),
         vmem((2, nz, nx, cap, wa), BF16),
         vmem((2, nz, nx, cap, wb), BF16),
@@ -477,11 +564,20 @@
     ]
     scratch += [vmem((ns, chans, tok), BF16)] * 4
     scratch += [vmem((hidden, width), BF16)] * 3
+    few = chunk // 4
+    rest = chunk - few
+    ga = ne * rest * 5 // 24
+    gb = ne * rest // 2 - ga
     scratch += [
-        vmem((ne, cap, chunk), BF16),
-        vmem((ne, cap, chunk), BF16),
-        vmem((2, nz, nx, cap, wa), BF16),
-        vmem((2, nz, nx, cap, wb), BF16),
+        vmem((1, width), F32),
+        vmem((ne, cap, rest), BF16),
+        vmem((ne, cap, rest), BF16),
+        vmem((2, nz, nx, cap, ga), BF16),
+        vmem((2, nz, nx, cap, gb), BF16),
+        vmem((nz, nx, tok, few), BF16),
+        vmem((nz, nx, 8, tok), F32),
+        vmem((nz, ne, nx, cap, few), BF16),
+        vmem((nz, ne, nx, cap, few), BF16),
         vmem((2, nz - 1, nx, cap, wa), BF16),
         vmem((2, nx - 1, cap, wa), BF16),
         vmem((2, nx - 1, nz, cap, wb), BF16),
@@ -503,6 +599,7 @@
         dma((ne,)),
         dma((ne,)),
     ] + [dma((2,))] * 8
+    scratch += [dma((nz, nx)), dma((nz, nx)), dma((nz,)), dma, dma((2,)), dma((2,))]
     return pl.pallas_call(
         functools.partial(block_kernel, (nz, nx, ne, cap, wa, wb)),
         out_shape=jax.ShapeDtypeStruct((tok, chunk), F32),

time: 176 us -> 171 us (0.972)
  Pallas kernels: 174 us -> 170 us
    pallas_call x1, Pallas kernels: 174 us -> 170 us  [block(): pl.pallas_call(functools.partial(block_kernel, (nz, nx, ne, cap, wa, wb))...]
where the time goes in v5:
time: 171 us
  Pallas kernels  170 us (99%)
    pallas_call x1, Pallas kernels, block(): pl.pallas_call(functools.partial(block_kernel, (nz, nx, ne, cap, wa, wb))...  170 us

profile of v5, /device:TPU:1, one launch (start us, length us, event | category | flops | bytes accessed | tf_op | source)
XLA Modules:
  0.0 171.2 jit_solution(1515577095216399221)
XLA Ops:
  0.0 169.5 %shard_map.127 = f32[128,512]{1,0:T(8,128)} custom-call(bf16[128,512]{1,0:T(8,128)(2,1)} %res_ref.1, bf16[128,512]{1,0:T(8,128)(2,1)} %q_ref.1, bf16[128,512]{1,0:T(8,128)(2,1)} %k_ref.1, bf16[128,512]{1,0:T(8,128)(2,1)} %v_ref.1, f32[3,3,512]{2,1,0:T(4,128)} %filt_ref.1, f32[16,4096]{1,0:T(8,128)} %bitcast.10, f32[1,16]{1,0:T(1,128)} %decay_ref.1, ...), custom_call_target="tpu_custom_call" | custom-call | tf_op jit(solution)/shard_map/pallas_call | solution.py:603
  169.5 1.6 convert_element_type.3
